TPU v7x, 32 devices: a whole 2x2x4 slice. The times are simulated.
32 devices in a mesh: img: 8 (over z, x), win: 4 (over y, core).
Axes of the slice: x: 2, y: 2, z: 4, core: 2. Of those that a mesh axis runs over, the one named last changes fastest.
Arguments:
- inputs: bfloat16 [32, 4, 256, 512], P('img', 'win'), may hold values from -6 to 6
- query_key_value_weight: bfloat16 [512, 1536], replicated, may hold values from -0.25 to 0.25
- query_bias: float32 [512], replicated, may hold values from -3 to 3
- value_bias: float32 [512], replicated, may hold values from -3 to 3
- head_log_scale: float32 [16], replicated, may hold values from 1 to 2.5
- bias_net_first_weight: float32 [2, 512], replicated, may hold values from -5 to 5
- bias_net_first_bias: float32 [512], replicated, may hold values from -3 to 3
- bias_net_second_weight: float32 [512, 16], replicated, may hold values from -0.25 to 0.25
- attention_out_weight: bfloat16 [512, 512], replicated, may hold values from -0.25 to 0.25
- attention_out_bias: float32 [512], replicated, may hold values from -2 to 2
- attention_norm_gain: float32 [512], replicated, may hold values from 0.5 to 1.5
- attention_norm_bias: float32 [512], replicated, may hold values from -2 to 2
- expand_weight: bfloat16 [512, 2048], replicated, may hold values from -0.25 to 0.25
- expand_bias: float32 [2048], replicated, may hold values from -2 to 2
- contract_weight: bfloat16 [2048, 512], replicated, may hold values from -0.125 to 0.125
- contract_bias: float32 [512], replicated, may hold values from -2 to 2
- feedforward_norm_gain: float32 [512], replicated, may hold values from 0.5 to 1.5
- feedforward_norm_bias: float32 [512], replicated, may hold values from -2 to 2
- cotangent: bfloat16 [32, 4, 256, 512], P('img', 'win'), may hold values from -6 to 6
Outputs:
- result: bfloat16 [32, 4, 256, 512], P('img', 'win')
- grad_inputs: bfloat16 [32, 4, 256, 512], P('img', 'win')
- grad_w_qkv: float32 [512, 1536], replicated
- grad_q_bias: float32 [512], replicated
- grad_v_bias: float32 [512], replicated
- grad_logit_scale: float32 [16], replicated
- gradient_net_first_weight: float32 [2, 512], replicated
- gradient_net_first_bias: float32 [512], replicated
- gradient_net_second_weight: float32 [512, 16], replicated
- grad_w_proj: float32 [512, 512], replicated
- grad_b_proj: float32 [512], replicated
- grad_ln1_gain: float32 [512], replicated
- grad_ln1_bias: float32 [512], replicated
- grad_w_fc1: float32 [512, 2048], replicated
- grad_b_fc1: float32 [2048], replicated
- grad_w_fc2: float32 [2048, 512], replicated
- grad_b_fc2: float32 [512], replicated
- grad_ln2_gain: float32 [512], replicated
- grad_ln2_bias: float32 [512], replicated
All inputs are finite; a program needn't handle non-finite values.
Results may differ from a plain program's by a relative error of at most 0.03.
Values may be sent and summed in bfloat16 or wider, within the bound.
A program may use at most 256 MiB of HBM per device.

v0:
```python
import functools

import jax
import jax.numpy as jnp
import numpy as np
from jax import lax
from jax.experimental import pallas as pl
from jax.experimental.pallas import tpu as pltpu
from jax.sharding import PartitionSpec as P

WIN = 16
TOK = WIN * WIN
EPS_DIR = 1e-06
EPS_NORM = 1e-05
MASK_FILL = -100.0
BIAS_RANGE = 16.0
INV_ROOT_TWO = 0.7071067811865476
INV_ROOT_TWOPI = 0.3989422804014327
MESH = pl.DeviceIdType.MESH
BF = jnp.bfloat16
F32 = jnp.float32

(ROW_QB, ROW_VB, ROW_LS, ROW_W1, ROW_B1, ROW_W2, ROW_BP, ROW_G1, ROW_S1, ROW_B2, ROW_G2, ROW_S2,
 ROW_BE, SMALL_ROWS) = (0, 1, 2, 3, 5, 6, 22, 23, 24, 25, 26, 27, 28, 32)


def nn(a, b):
    return lax.dot_general(a, b, (((1,), (0,)), ((), ())), preferred_element_type=F32)


def nt(a, b):
    return lax.dot_general(a, b, (((1,), (1,)), ((), ())), preferred_element_type=F32)


def tn(a, b):
    return lax.dot_general(a, b, (((0,), (0,)), ((), ())), preferred_element_type=F32)


def split3(v):
    hi = v.astype(BF)
    rest = v - hi.astype(F32)
    mid = rest.astype(BF)
    return hi, mid, (rest - mid.astype(F32)).astype(BF)


def gelu_parts(v):
    ex = jnp.exp(-0.5 * v * v)
    d = 1.0 + (0.3275911 * INV_ROOT_TWO) * jnp.abs(v)
    t = pl.reciprocal(d, approx=True)
    t = t * (2.0 - d * t)
    poly = t * (
        0.127414796 + t * (-0.142248368 + t * (0.7107068705 + t * (-0.7265760135 + t * 0.5307027145)))
    )
    tail = poly * ex
    return jnp.where(v >= 0.0, 1.0 - tail, tail), ex * INV_ROOT_TWOPI


def col_sum(v):
    return jnp.sum(v.reshape(v.shape[0] // 8, 8, v.shape[1]), axis=0)


def to_blocks(v):
    n = v.shape[-1]
    t = v.reshape(2, 8, 2, 8, n)
    return [[t[qr, :, qc].reshape(64, n) for qc in range(2)] for qr in range(2)]


def from_blocks(quads):
    n = quads[0][0].shape[-1]
    rows = []
    for qr in range(2):
        a = quads[qr][0].reshape(8, 1, 8, n)
        b = quads[qr][1].reshape(8, 1, 8, n)
        rows.append(jnp.concatenate([a, b], axis=1).reshape(128, n))
    return jnp.concatenate(rows, axis=0)


def one_hot_places(c):
    l = lax.broadcasted_iota(jnp.int32, (256, 512), 0)
    k = lax.broadcasted_iota(jnp.int32, (256, 512), 1) + 512 * c
    return jnp.where(l == 8 * (15 - k // 128) + k % 128, 1.0, 0.0).astype(BF)


def one_hot_pick():
    k = lax.broadcasted_iota(jnp.int32, (1024, 256), 0)
    l = lax.broadcasted_iota(jnp.int32, (1024, 256), 1)
    return jnp.where(k == 32 * (l // 8) + l % 8, 1.0, 0.0).astype(BF)


def table_coords():
    k = np.arange(1024)
    out = np.zeros((2, 1024), np.float64)
    for i, off in enumerate((15 - k // 32, 15 - k % 32)):
        u = off * (8.0 / 15.0)
        out[i] = np.sign(u) * np.log2(np.abs(u) + 1.0) / 3.0
    rows = np.zeros((8, 1024), np.float32)
    rows[0:2] = out
    rows[2] = 1.0
    cols = np.zeros((1024, 8), np.float32)
    cols[:, 0:2] = out.T
    return rows, cols


def net_first(cols, w1, b1):
    return cols[:, 0:1] * w1[0:1, :] + cols[:, 1:2] * w1[1:2, :] + b1


def block_kernel(
    n_img, n_win,
    x_hbm, cot_hbm, wqkv, wproj, we, wc, qb, vb, hls, w1, b1, w2t, bproj, g1, s1, be, bc, g2, s2,
    crow, ccol,
    res_hbm, gin_hbm, sums_hbm, small_out,
    xr, cr, xroll, bias, ex, qs, kl, vl, qinv, kinv, isum, mixed, mixlo, blk, dmid, act, dhid, dout,
    mlow, slope, tab, part, acc_s, asum, rcore, rone, rtwo, rz, own, small_s, small_r,
    s_x, r_x, s_c, r_c, s_res, r_res, s_gin, r_gin, s_ar, r_ar, l_ar, s_sm, r_sm,
):
    img = lax.axis_index("img")
    me = lax.axis_index("win")
    extra = n_img // 8
    core = lax.rem(me, 2)
    ypos = me // 2
    xpos = lax.rem(img, 2)
    zpos = lax.rem(img // 2, 4)
    upper = img // 8

    def ring_to(k):
        return (img, lax.rem(me + k, n_win))

    def ring_from(k):
        return lax.rem(me + n_win - k, n_win)

    core_peer = (img, me + 1 - 2 * core)
    y_peer = (img, lax.rem(me + 2, 4))
    x_peer = (img + 1 - 2 * xpos, me)

    def z_peer(k):
        return (upper * 8 + lax.rem(zpos + k, 4) * 2 + xpos, me)

    def far_peer(k):
        return (lax.rem(upper + k, extra) * 8 + zpos * 2 + xpos, me)

    barrier = pltpu.get_barrier_semaphore()
    others = [ring_to(k) for k in range(1, n_win)] + [x_peer]
    others += [z_peer(k) for k in range(1, 4)] + [far_peer(k) for k in range(1, extra)]
    for peer in others:
        pl.semaphore_signal(barrier, inc=1, device_id=peer, device_id_type=MESH)
    pl.semaphore_wait(barrier, len(others))

    def remote(src, dst, ssem, rsem, peer):
        return pltpu.make_async_remote_copy(
            src_ref=src, dst_ref=dst, send_sem=ssem, recv_sem=rsem, device_id=peer, device_id_type=MESH
        )

    def spread(src_hbm, dst, ssem, rsem, k):
        to = lax.rem(me + k, n_win)
        return remote(src_hbm.at[to, 0], dst.at[me], ssem.at[k], rsem.at[k], ring_to(k))

    def spread_in(src_hbm, dst, ssem, rsem, k):
        frm = ring_from(k)
        return remote(src_hbm.at[frm, 0], dst.at[frm], ssem.at[k], rsem.at[k], ring_to(k))

    def own_part(src_hbm, dst, sem):
        return pltpu.make_async_copy(src_hbm.at[me, 0], dst.at[me], sem.at[0])

    for k in (2, 1, 3):
        spread(x_hbm, xr, s_x, r_x, k).start()
    own_part(x_hbm, xr, r_x).start()

    def net_piece(c):
        rows = pl.ds(pl.multiple_of(256 * c, 256), 256)
        return rows, net_first(ccol[rows, :], w1[...], b1[...][None, :])

    def look_up(c, _):
        cols, pre = net_piece(c)
        logits = lax.dot_general(
            w2t[...], pre * gelu_parts(pre)[0], (((1,), (1,)), ((), ())),
            precision=lax.Precision.HIGHEST, preferred_element_type=F32,
        )
        tab[:, cols] = BIAS_RANGE / (1.0 + jnp.exp(-logits))
        return 0

    lax.fori_loop(0, 4, look_up, 0)
    for u in range(24):
        part[:, u, :] = pltpu.roll(tab[...], 1001 + u, 1)
    pick = one_hot_pick()
    short = jnp.concatenate(
        [sum(nn(p, pick) for p in split3(part[4 * i : 4 * i + 4].reshape(96, 1024))) for i in range(4)], axis=0
    )
    short_parts = split3(short)
    for c in range(4):
        places = one_hot_places(c)
        wide = sum(nn(p, places) for p in short_parts)
        for r in range(4):
            row = 8 * (4 * c + r)
            bias[:, :, row : row + 8, :] = wide[:, 128 * r : 128 * r + 128].reshape(16, 3, 8, 128)

    lane = lax.broadcasted_iota(jnp.int32, (1, 128), 1)
    head_mask = [jnp.where(lane // 32 == hh, 1.0, 0.0).astype(BF) for hh in range(4)]
    l0 = lax.broadcasted_iota(jnp.int32, (256, 256), 0)
    l1 = lax.broadcasted_iota(jnp.int32, (256, 256), 1)
    head_ones = jnp.where(l0 // 32 == l1 // 32, 1.0, 0.0).astype(BF)

    def scale_lanes(p):
        wide = lax.broadcasted_iota(jnp.int32, (1, 256), 1) // 32
        out = jnp.zeros((1, 256), F32)
        for i in range(8):
            out = jnp.where(wide == i, hls[8 * p + i], out)
        return jnp.exp(out)

    for k in (0, 1, 2, 3):
        if k == 0:
            own_part(x_hbm, xr, r_x).wait()
        else:
            spread_in(x_hbm, xr, s_x, r_x, k).wait_recv()
    for k in (2, 1, 3):
        spread(cot_hbm, cr, s_c, r_c, k).start()
    own_part(cot_hbm, cr, r_c).start()

    def lay(w, _):
        quads = to_blocks(xr[w].astype(F32))
        for qr in range(2):
            for qc in range(2):
                br, bcol = 1 - qr, 1 - qc
                orow = w // 2 if br == 0 else 1 - w // 2
                ocol = lax.rem(w, 2) if bcol == 0 else 1 - lax.rem(w, 2)
                at = (bcol * 2 + br) * 64
                xroll[2 * orow + ocol, at : at + 64, :] = quads[qr][qc].astype(BF)
        return 0

    lax.fori_loop(0, 4, lay, 0)

    row_half = lax.broadcasted_iota(jnp.int32, (128, 128), 0) // 64
    col_half = lax.broadcasted_iota(jnp.int32, (128, 128), 1) // 64
    apart = jnp.where(row_half == col_half, 0.0, MASK_FILL)

    def home(o, bcol, br):
        return lax.rem(2 * (o // 2) + br + 1, 4), lax.rem(2 * lax.rem(o, 2) + bcol + 1, 4)

    def attend(o, _):
        xw = xroll[o]
        for p in range(2):
            cols = slice(256 * p, 256 * p + 256)
            q = nn(xw, wqkv[:, cols]) + qb[cols][None, :]
            qi = lax.rsqrt(nn((q * q).astype(BF), head_ones) + EPS_DIR)
            qsc = (q * qi * scale_lanes(p)).astype(BF)
            k = nn(xw, wqkv[:, 512 + 256 * p : 768 + 256 * p])
            ki = lax.rsqrt(nn((k * k).astype(BF), head_ones) + EPS_DIR)
            kn = (k * ki).astype(BF)
            v = (nn(xw, wqkv[:, 1024 + 256 * p : 1280 + 256 * p]) + vb[cols][None, :]).astype(BF)
            for i in range(2):
                half = slice(128 * i, 128 * i + 128)
                qs[o, 2 * p + i] = qsc[:, half]
                kl[o, 2 * p + i] = kn[:, half]
                vl[o, 2 * p + i] = v[:, half]
                qinv[o, 2 * p + i] = qi[:, half].astype(BF)
                kinv[o, 2 * p + i] = ki[:, half].astype(BF)
        rows_cut = jnp.where(o // 2 == 1, apart, 0.0)
        cols_cut = jnp.where(lax.rem(o, 2) == 1, jnp.full((128, 128), MASK_FILL, F32), rows_cut)

        for g in range(4):
            qg, kg, vg = qs[o, g], kl[o, g], vl[o, g]
            total = jnp.zeros((256, 256), F32)
            for hh in range(4):
                h = 4 * g + hh
                sc = nt(qg * head_mask[hh], kg)
                ex[o, g, hh, 0:128, 0:128] = jnp.exp(sc[0:128, 0:128] + bias[h, 1] + rows_cut).astype(BF)
                ex[o, g, hh, 0:128, 128:256] = jnp.exp(sc[0:128, 128:256] + bias[h, 0] + cols_cut).astype(BF)
                ex[o, g, hh, 128:256, 0:128] = jnp.exp(sc[128:256, 0:128] + bias[h, 2] + cols_cut).astype(BF)
                ex[o, g, hh, 128:256, 128:256] = jnp.exp(sc[128:256, 128:256] + bias[h, 1] + rows_cut).astype(BF)
                ones = jnp.broadcast_to(head_mask[hh], (256, 128))
                total = total + nn(ex[o, g, hh], jnp.concatenate([vg * head_mask[hh], ones], axis=1))
            inv = 1.0 / total[:, 128:256]
            isum[o, g] = inv
            mix = total[:, 0:128] * inv
            mix_hi = mix.astype(BF)
            mixed[o, :, 128 * g : 128 * g + 128] = mix_hi
            mixlo[o, :, 128 * g : 128 * g + 128] = (mix - mix_hi.astype(F32)).astype(BF)

        branch = (nn(mixed[o], wproj[...]) + bproj[...][None, :]).astype(BF)
        for bcol in range(2):
            for br in range(2):
                at = (bcol * 2 + br) * 64
                brow, bc_ = home(o, bcol, br)
                blk[brow, bc_] = branch[at : at + 64, :]
        return 0

    lax.fori_loop(0, 4, attend, 0)

    for k in (0, 1, 2, 3):
        if k == 0:
            own_part(cot_hbm, cr, r_c).wait()
        else:
            spread_in(cot_hbm, cr, s_c, r_c, k).wait_recv()
    acc_s[...] = jnp.zeros_like(acc_s)

    def res_copy(w):
        return remote(xr.at[w], res_hbm.at[me, 0], s_res.at[w], r_res.at[me], (img, w))

    def dense(w, _):
        wr, wcol = w // 2, lax.rem(w, 2)

        def flat(quads):
            return jnp.concatenate([quads[0][0], quads[0][1], quads[1][0], quads[1][1]], axis=0)

        x = flat(to_blocks(xr[w].astype(F32)))
        e = flat(to_blocks(cr[w].astype(F32)))
        back = jnp.concatenate(
            [blk[2 * wr + qr, 2 * wcol + qc] for qr in range(2) for qc in range(2)], axis=0
        ).astype(F32)
        ctr = back - jnp.mean(back, axis=1, keepdims=True)
        r1 = lax.rsqrt(jnp.mean(ctr * ctr, axis=1, keepdims=True) + EPS_NORM)
        z1 = ctr * r1
        middle = x + z1 * g1[...][None, :] + s1[...][None, :]
        ml = middle.astype(BF)
        rows = pl.ds(pl.multiple_of(w * TOK, TOK), TOK)
        mlow[rows, :] = ml
        out = jnp.zeros((TOK, 512), F32)
        for c in range(4):
            cols = slice(512 * c, 512 * c + 512)
            hid = nn(ml, we[:, cols]) + be[cols][None, :]
            cap, low = gelu_parts(hid)
            a = (hid * cap).astype(BF)
            act[c, rows, :] = a
            slope[c] = (cap + hid * low).astype(BF)
            out = out + nn(a, wc[cols, :])
        out = out + bc[...][None, :]
        ctr2 = out - jnp.mean(out, axis=1, keepdims=True)
        r2 = lax.rsqrt(jnp.mean(ctr2 * ctr2, axis=1, keepdims=True) + EPS_NORM)
        z2 = ctr2 * r2
        result = middle + z2 * g2[...][None, :] + s2[...][None, :]
        quads = [[result[128 * qr + 64 * qc : 128 * qr + 64 * qc + 64] for qc in range(2)] for qr in range(2)]
        xr[w] = from_blocks(quads).astype(BF)

        @pl.when(w != me)
        def _():
            res_copy(w).start()

        acc_s[0] += col_sum(e * z2)
        acc_s[1] += col_sum(e)
        dn = e * g2[...][None, :]
        dv = r2 * (
            dn - jnp.mean(dn, axis=1, keepdims=True) - z2 * jnp.mean(dn * z2, axis=1, keepdims=True)
        )
        do = dv.astype(BF)
        dout[rows, :] = do
        acc_s[2] += col_sum(do.astype(F32))
        dm = e
        for c in range(4):
            cols = slice(512 * c, 512 * c + 512)
            dh = (nt(do, wc[cols, :]) * slope[c].astype(F32)).astype(BF)
            dhid[c, rows, :] = dh
            acc_s[3 + c] += col_sum(dh.astype(F32))
            dm = dm + nt(dh, we[:, cols])
        acc_s[7] += col_sum(dm * z1)
        acc_s[8] += col_sum(dm)
        dn1 = dm * g1[...][None, :]
        db = r1 * (
            dn1 - jnp.mean(dn1, axis=1, keepdims=True) - z1 * jnp.mean(dn1 * z1, axis=1, keepdims=True)
        )
        db = db.astype(BF)
        for qr in range(2):
            for qc in range(2):
                at = 128 * qr + 64 * qc
                dmid[2 * wr + qr, 2 * wcol + qc] = dm[at : at + 64]
                blk[2 * wr + qr, 2 * wcol + qc] = db[at : at + 64]
        return 0

    lax.fori_loop(0, 4, dense, 0)
    own_res = pltpu.make_async_copy(xr.at[me], res_hbm.at[me, 0], r_res.at[me])
    own_res.start()

    def rows_of(c, s=0, b1=None, b2=None, z=None):
        at, size = 0, 1024
        if b1 is not None:
            at, size = at + s * 512 + b1 * 256, 256
        if b2 is not None:
            at, size = at + b2 * 128, 128
        if z is not None:
            at, size = at + z * 32, 32
        return c, pl.ds(pl.multiple_of(at, 32), size)

    first = (xpos, ypos)
    second = (ypos, xpos)
    first_peer = (x_peer, y_peer)
    second_peer = (y_peer, x_peer)

    def sum_plan(a, src, rcore):
        full = sums_hbm.at[a]

        def sems(i):
            return s_ar.at[a, i], r_ar.at[a, i]

        def core_send():
            return remote(src.at[rows_of(1 - core)], rcore, *sems(0), core_peer)

        def one_send(s):
            return remote(src.at[rows_of(core, s, 1 - first[s])], rone.at[a, s], *sems(1 + s), first_peer[s])

        def two_send(s):
            return remote(
                src.at[rows_of(core, s, first[s], 1 - second[s])], rtwo.at[a, s], *sems(3 + s), second_peer[s]
            )

        def z_send(s, k):
            return remote(
                src.at[rows_of(core, s, first[s], second[s], lax.rem(zpos + k, 4))],
                rz.at[a, s, k - 1], *sems(5 + 3 * s + k - 1), z_peer(k),
            )

        def far_send(s, k):
            return remote(
                own.at[a, s, 0], own.at[a, s, k], *sems(22 + (extra - 1) * s + k - 1), far_peer(k)
            )

        def out_z(s, k, z):
            at = rows_of(core, s, first[s], second[s], z)
            return remote(own.at[a, s, extra], full.at[at], *sems(11 + 3 * s + k - 1), z_peer(k))

        def out_own(s):
            at = rows_of(core, s, first[s], second[s], zpos)
            return pltpu.make_async_copy(own.at[a, s, extra], full.at[at], l_ar.at[a, s])

        def out_two(s, b2):
            at = rows_of(core, s, first[s], b2)
            return remote(full.at[at], full.at[at], *sems(17 + s), second_peer[s])

        def out_one(s, b1):
            at = rows_of(core, s, b1)
            return remote(full.at[at], full.at[at], *sems(19 + s), first_peer[s])

        def out_core(c):
            at = rows_of(c)
            return remote(full.at[at], full.at[at], *sems(21), core_peer)

        def step0():
            core_send().start()

        def step1():
            core_send().wait_recv()
            at = rows_of(core)
            src[at] = src[at] + rcore[...]
            for s in range(2):
                one_send(s).start()

        def step2():
            for s in range(2):
                one_send(s).wait_recv()
                at = rows_of(core, s, first[s])
                src[at] = src[at] + rone[a, s]
                two_send(s).start()

        def step3():
            for s in range(2):
                two_send(s).wait_recv()
                at = rows_of(core, s, first[s], second[s])
                src[at] = src[at] + rtwo[a, s]
                for k in (2, 1, 3):
                    z_send(s, k).start()

        def step4():
            for s in range(2):
                for k in (1, 2, 3):
                    z_send(s, k).wait_recv()
                at = rows_of(core, s, first[s], second[s], zpos)
                total = src[at].astype(F32)
                for k in range(3):
                    total = total + rz[a, s, k].astype(F32)
                own[a, s, 0] = total.astype(BF)
                for k in range(1, extra):
                    far_send(s, k).start()
            for s in range(2):
                total = own[a, s, 0].astype(F32)
                for k in range(1, extra):
                    far_send(s, k).wait_recv()
                    total = total + own[a, s, k].astype(F32)
                own[a, s, extra] = total.astype(BF)
                out_own(s).start()
                for k in (2, 1, 3):
                    out_z(s, k, zpos).start()

        def step5():
            for s in range(2):
                out_own(s).wait()
                for k in (1, 2, 3):
                    out_z(s, k, lax.rem(zpos + 4 - k, 4)).wait_recv()
                out_two(s, second[s]).start()

        def step6():
            for s in range(2):
                out_two(s, 1 - second[s]).wait_recv()
                out_one(s, first[s]).start()

        def step7():
            for s in range(2):
                out_one(s, 1 - first[s]).wait_recv()
            out_core(core).start()

        def step8():
            out_core(1 - core).wait_recv()
            core_send().wait_send()
            for s in range(2):
                one_send(s).wait_send()
                two_send(s).wait_send()
                out_two(s, second[s]).wait_send()
                out_one(s, first[s]).wait_send()
                for k in (1, 2, 3):
                    z_send(s, k).wait_send()
                    out_z(s, k, zpos).wait_send()
                for k in range(1, extra):
                    far_send(s, k).wait_send()
            out_core(core).wait_send()

        return [step0, step1, step2, step3, step4, step5, step6, step7, step8]

    plan_two = sum_plan(0, asum.at[0], rcore.at[0])
    plan_one = sum_plan(1, asum.at[1], rcore.at[1])
    plan_tail = sum_plan(2, act.at[0:2], act.at[2])

    for c in range(4):
        asum[0, c // 2, 512 * (c % 2) : 512 * (c % 2) + 512, :] = tn(act[c], dout[...]).astype(BF)
    plan_two[0]()
    for c in range(4):
        asum[1, c // 2, 512 * (c % 2) : 512 * (c % 2) + 512, :] = tn(mlow[...], dhid[c]).astype(BF)
    plan_one[0]()

    bias[...] = jnp.zeros_like(bias)
    acc_s[9] = jnp.zeros((8, 512), F32)

    def gather(o, _):
        for bcol in range(2):
            for br in range(2):
                at = (bcol * 2 + br) * 64
                brow, bc_ = home(o, bcol, br)
                cr[o, at : at + 64, :] = blk[brow, bc_]
        return 0

    lax.fori_loop(0, 4, gather, 0)
    head_ones_half = head_ones[0:128, 0:128]
    minus = jnp.full((256, 128), -1.0, BF)
    lane32 = lax.rem(lax.broadcasted_iota(jnp.int32, (256, 128), 1), 32)

    slots = {}
    for at, step in zip((0, 3, 5, 8, 11, 13, 15), plan_two[1:8]):
        slots.setdefault(at, []).append(step)
    for at, step in zip((1, 6, 9, 12, 15), plan_one[1:6]):
        slots.setdefault(at, []).append(step)

    def retreat(o, _):
        dmx = nt(cr[o], wproj[...])
        rows = pl.ds(pl.multiple_of(o * TOK, TOK), TOK)
        for g in range(4):
            lanes = slice(128 * g, 128 * g + 128)
            qg, kg, vg = qs[o, g], kl[o, g], vl[o, g]
            dmg = dmx[:, lanes] * isum[o, g]
            dmp = dmg.astype(BF)
            mix = mixed[o, :, lanes].astype(F32) + mixlo[o, :, lanes].astype(F32)
            prod = dmp.astype(F32) * mix
            delta = sum(nn(p, head_ones_half) for p in split3(prod)[:2])
            delta_hi, delta_lo, _ = split3(delta)
            prod = jnp.where(lane32 == 0, delta_hi, jnp.where(lane32 == 1, delta_lo, jnp.zeros_like(delta_lo)))
            vw = jnp.concatenate([vg, minus], axis=1)
            dmp_t = dmg.T.astype(BF)
            qg_t = qg.astype(F32).T.astype(BF)
            dq = jnp.zeros((256, 128), F32)
            dk_t, dv_t = [], []
            for hh in range(4):
                h = 4 * g + hh
                mask = head_mask[hh]
                left = jnp.concatenate([dmp * mask, prod * mask], axis=1)
                eh = ex[o, g, hh]
                dsf = nt(left, vw) * eh.astype(F32)
                ds = dsf.astype(BF)
                bias[h, 1] += dsf[0:128, 0:128] + dsf[128:256, 128:256]
                bias[h, 0] += dsf[0:128, 128:256]
                bias[h, 2] += dsf[128:256, 0:128]
                dq = dq + nn(ds, kg * mask)
                dk_t.append(nn(qg_t[32 * hh : 32 * hh + 32], ds))
                dv_t.append(nn(dmp_t[32 * hh : 32 * hh + 32], eh))
            dk = jnp.concatenate(dk_t, axis=0).T
            dv = jnp.concatenate(dv_t, axis=0).T
            qf, kf = qg.astype(F32), kg.astype(F32)
            scale = scale_lanes(g // 2)[:, 128 * (g % 2) : 128 * (g % 2) + 128]
            tq = dq * qf
            acc_s[9, :, lanes] += col_sum(tq)
            aq = nn(tq.astype(BF), head_ones_half)
            ak = nn((dk * kf).astype(BF), head_ones_half)
            dhid[0, rows, lanes] = (qinv[o, g].astype(F32) * (scale * dq - (1.0 / scale) * qf * aq)).astype(BF)
            dhid[1, rows, lanes] = (kinv[o, g].astype(F32) * (dk - kf * ak)).astype(BF)
            dhid[2, rows, lanes] = dv.astype(BF)
            for at, steps in slots.items():
                if at % 4 == g:

                    @pl.when(o == at // 4)
                    def _(steps=steps):
                        for step in steps:
                            step()

        moved = sum(nt(dhid[i, rows, :], wqkv[:, 512 * i : 512 * i + 512]) for i in range(3))
        for bcol in range(2):
            for br in range(2):
                at = (bcol * 2 + br) * 64
                brow, bc_ = home(o, bcol, br)
                dmid[brow, bc_] += moved[at : at + 64, :]
        return 0

    lax.fori_loop(0, 4, retreat, 0)

    xflat = xroll[...].reshape(1024, 512)
    for i in range(3):
        act[i // 2, 512 * (i % 2) : 512 * (i % 2) + 512, :] = tn(xflat, dhid[i]).astype(BF)
    act[1, 512:1024, :] = tn(mixed[...].reshape(1024, 512), cr[...].reshape(1024, 512)).astype(BF)
    plan_tail[0]()

    def gin_copy(w):
        return remote(slope.at[w], gin_hbm.at[me, 0], s_gin.at[w], r_gin.at[me], (img, w))

    def finish(w, _):
        wr, wcol = w // 2, lax.rem(w, 2)
        quads = [[dmid[2 * wr + qr, 2 * wcol + qc] for qc in range(2)] for qr in range(2)]
        slope[w] = from_blocks(quads).astype(BF)

        @pl.when(w != me)
        def _():
            gin_copy(w).start()

        return 0

    lax.fori_loop(0, 4, finish, 0)
    own_gin = pltpu.make_async_copy(slope.at[me], gin_hbm.at[me, 0], r_gin.at[me])
    own_gin.start()
    plan_one[6]()
    plan_tail[1]()

    row_ones = jnp.ones((8, 1024), BF)

    def put(row, v):
        small_s[0, row : row + v.shape[0], :] = v

    put(ROW_QB, nn(row_ones, dhid[0])[0:1])
    put(ROW_VB, nn(row_ones, dhid[2])[0:1])
    put(ROW_BP, nn(row_ones, cr[...].reshape(1024, 512))[0:1])
    for row, i in ((ROW_LS, 9), (ROW_G1, 7), (ROW_S1, 8), (ROW_B2, 2), (ROW_G2, 0), (ROW_S2, 1)):
        put(row, jnp.sum(acc_s[i], axis=0, keepdims=True))
    for c in range(4):
        put(ROW_BE + c, jnp.sum(acc_s[3 + c], axis=0, keepdims=True))
    short = jnp.zeros((384, 256), F32)
    for c in range(4):
        places = one_hot_places(c)
        left = jnp.concatenate(
            [bias[:, :, 8 * r : 8 * r + 8, :].reshape(384, 128) for r in range(4 * c, 4 * c + 4)], axis=1
        )
        for p in split3(left)[:2]:
            short = short + nt(p, places)
    pick = one_hot_pick()
    for i in range(4):
        piece = split3(short[96 * i : 96 * i + 96])[:2]
        part[4 * i : 4 * i + 4] = sum(nt(p, pick) for p in piece).reshape(4, 24, 1024)
    plan_tail[2]()
    dtab = jnp.zeros((16, 1024), F32)
    for u in range(24):
        dtab = dtab + pltpu.roll(part[:, u, :], 23 - u, 1)
    tab[...] = dtab * tab[...] * (1.0 - tab[...] * (1.0 / BIAS_RANGE))
    small_s[0, ROW_W1 : ROW_W2 + 16, :] = jnp.zeros((ROW_W2 + 16 - ROW_W1, 512), F32)

    def net_back(c, _):
        cols, pre = net_piece(c)
        cap, low = gelu_parts(pre)
        dlog, dlog_lo, _ = split3(tab[:, cols])
        units, units_lo, _ = split3(pre * cap)
        small_s[0, ROW_W2 : ROW_W2 + 16, :] += nn(dlog, units) + nn(dlog_lo, units) + nn(dlog, units_lo)
        w_hi, w_lo, _ = split3(w2t[...])
        back = tn(dlog, w_hi) + tn(dlog_lo, w_hi) + tn(dlog, w_lo)
        dpre, dpre_lo, _ = split3(back * (cap + pre * low))
        hi, mid, _ = split3(crow[:, cols])
        net = nn(hi, dpre) + nn(mid, dpre) + nn(hi, dpre_lo)
        small_s[0, ROW_W1 : ROW_W1 + 3, :] += net[0:3]
        return 0

    lax.fori_loop(0, 4, net_back, 0)
    plan_one[7]()
    plan_two[8]()
    plan_tail[3]()

    stages = [[core_peer], [y_peer], [x_peer], [z_peer(k) for k in range(1, 4)]]
    if extra > 1:
        stages.append([far_peer(k) for k in range(1, extra)])
    later = [plan_tail[4], plan_tail[5], plan_one[8], plan_tail[6], plan_tail[7]]
    slot = 0
    for i, peers in enumerate(stages):
        copies = [
            remote(small_s.at[i], small_r.at[slot + j], s_sm.at[slot + j], r_sm.at[slot + j], peer)
            for j, peer in enumerate(peers)
        ]
        slot += len(peers)
        for c in copies:
            c.start()
        if i < len(later):
            later[i]()
        total = small_s[i]
        for j, c in enumerate(copies):
            c.wait()
            total = total + small_r[slot - len(peers) + j]
        small_s[i + 1] = total
    for step in later[len(stages) :]:
        step()
    plan_tail[8]()
    small_out[...] = small_s[len(stages)]

    own_res.wait()
    own_gin.wait()
    for k in (1, 2, 3):
        frm, to = ring_from(k), lax.rem(me + k, n_win)
        spread(x_hbm, xr, s_x, r_x, k).wait_send()
        spread(cot_hbm, cr, s_c, r_c, k).wait_send()
        res_copy(to).wait_send()
        gin_copy(to).wait_send()
        remote(xr.at[frm], res_hbm.at[frm, 0], s_res.at[frm], r_res.at[frm], (img, frm)).wait_recv()
        remote(slope.at[frm], gin_hbm.at[frm, 0], s_gin.at[frm], r_gin.at[frm], (img, frm)).wait_recv()


def body(n_img, n_win, inputs, wqkv, qb, vb, hls, w1, b1, w2, wproj, bproj, g1, s1, we, be, wc, bc, g2, s2, cot):
    extra = n_img // 8
    crow, ccol = table_coords()
    dma = pltpu.SemaphoreType.DMA
    n_ar = 22 + 2 * (extra - 1)
    n_sm = 6 + (extra - 1)
    vmem = pl.BlockSpec(memory_space=pltpu.VMEM)
    hbm = pl.BlockSpec(memory_space=pl.ANY)
    smem = pl.BlockSpec(memory_space=pltpu.SMEM)
    scratch = [
        pltpu.VMEM((4, TOK, 512), BF),
        pltpu.VMEM((4, TOK, 512), BF),
        pltpu.VMEM((4, TOK, 512), BF),
        pltpu.VMEM((16, 3, 128, 128), F32),
        pltpu.VMEM((4, 4, 4, TOK, TOK), BF),
        pltpu.VMEM((4, 4, TOK, 128), BF),
        pltpu.VMEM((4, 4, TOK, 128), BF),
        pltpu.VMEM((4, 4, TOK, 128), BF),
        pltpu.VMEM((4, 4, TOK, 128), BF),
        pltpu.VMEM((4, 4, TOK, 128), BF),
        pltpu.VMEM((4, 4, TOK, 128), F32),
        pltpu.VMEM((4, TOK, 512), BF),
        pltpu.VMEM((4, TOK, 512), BF),
        pltpu.VMEM((4, 4, 64, 512), BF),
        pltpu.VMEM((4, 4, 64, 512), F32),
        pltpu.VMEM((4, 1024, 512), BF),
        pltpu.VMEM((4, 1024, 512), BF),
        pltpu.VMEM((1024, 512), BF),
        pltpu.VMEM((1024, 512), BF),
        pltpu.VMEM((4, TOK, 512), BF),
        pltpu.VMEM((16, 1024), F32),
        pltpu.VMEM((16, 24, 1024), F32),
        pltpu.VMEM((10, 8, 512), F32),
        pltpu.VMEM((2, 2, 1024, 512), BF),
        pltpu.VMEM((2, 1024, 512), BF),
        pltpu.VMEM((3, 2, 256, 512), BF),
        pltpu.VMEM((3, 2, 128, 512), BF),
        pltpu.VMEM((3, 2, 3, 32, 512), BF),
        pltpu.VMEM((3, 2, extra + 1, 32, 512), BF),
        pltpu.VMEM((6, SMALL_ROWS, 512), F32),
        pltpu.VMEM((n_sm, SMALL_ROWS, 512), F32),
        dma((4,)), dma((4,)), dma((4,)), dma((4,)),
        dma((4,)), dma((4,)), dma((4,)), dma((4,)),
        dma((3, n_ar)), dma((3, n_ar)), dma((3, 2)),
        dma((n_sm,)), dma((n_sm,)),
    ]
    block = jax.ShapeDtypeStruct(inputs.shape, BF)
    result, grad_inputs, sums, small = pl.pallas_call(
        functools.partial(block_kernel, n_img, n_win),
        out_shape=(
            block,
            block,
            jax.ShapeDtypeStruct((3, 2, 1024, 512), BF),
            jax.ShapeDtypeStruct((SMALL_ROWS, 512), F32),
        ),
        in_specs=[hbm, hbm] + [vmem] * 6 + [smem] + [vmem] * 12,
        out_specs=(hbm, hbm, hbm, vmem),
        scratch_shapes=scratch,
        compiler_params=pltpu.CompilerParams(
            collective_id=0, has_side_effects=True, vmem_limit_bytes=64 * 1024 * 1024
        ),
    )(
        inputs, cot, wqkv, wproj, we, wc, qb, vb, hls, w1, b1, w2.T, bproj, g1, s1, be, bc, g2, s2,
        jnp.asarray(crow), jnp.asarray(ccol),
    )
    sums = sums.astype(F32)
    fc2 = sums[0].reshape(2048, 512)
    fc1 = jnp.transpose(sums[1].reshape(4, 512, 512), (1, 0, 2)).reshape(512, 2048)
    qkv = jnp.transpose(sums[2].reshape(4, 512, 512)[:3], (1, 0, 2)).reshape(512, 1536)
    proj = sums[2, 1, 512:]
    return (
        result,
        grad_inputs,
        qkv,
        small[ROW_QB],
        small[ROW_VB],
        jnp.sum(small[ROW_LS].reshape(16, 32), axis=1),
        small[ROW_W1 : ROW_W1 + 2],
        small[ROW_B1],
        small[ROW_W2 : ROW_W2 + 16].T,
        proj,
        small[ROW_BP],
        small[ROW_G1],
        small[ROW_S1],
        fc1,
        small[ROW_BE : ROW_BE + 4].reshape(2048),
        fc2,
        small[ROW_B2],
        small[ROW_G2],
        small[ROW_S2],
    )


def solution(mesh):
    n_img, n_win = mesh.shape["img"], mesh.shape["win"]
    block = P("img", "win", None, None)
    return jax.shard_map(
        functools.partial(body, n_img, n_win),
        mesh=mesh,
        in_specs=(block,) + (P(),) * 17 + (block,),
        out_specs=(block, block) + (P(),) * 17,
        check_vma=False,
    )
```

profile of v0, /device:TPU:0, one launch (start us, length us, event | category | flops | bytes accessed | tf_op | source)
XLA Modules:
  0.0 201.6 jit_solution(3539388198993150379)
XLA Ops:
  0.7 168.8 %shard_map.348 = (bf16[4,1,256,512]{3,2,1,0:T(8,128)(2,1)}, bf16[4,1,256,512]{3,2,1,0:T(8,128)(2,1)}, bf16[3,2,1024,512]{3,2,1,0:T(8,128)(2,1)}, f32[32,512]{1,0:T(8,128)}) custom-call(bf16[4,1,256,512]{3,2,1,0:T(8,128)(2,1)} %x_hbm.1, bf16[4,1,256,512]{3,2,1,0:T(8,128)(2,1)} %cot_hbm.1, bf16[512,1536]{1,0:T(8,128)(2,1)} %wqkv.1, bf16[512,512]{1,0:T(8,128)(2,1)} %wproj.1, ...), custom_call_target="tpu_custom_call" | custom-call | tf_op jit(solution)/shard_map/pallas_call | solution.py:768
  169.5 0.0 slice-start
  169.5 1.5 slice.59
  171.0 0.7 slice_bitcast_fusion.2
  171.7 0.6 copy.47
  172.3 1.5 fusion.1
  173.8 1.4 slice_bitcast_fusion.1
  175.3 0.1 reshape_squeeze.13
  175.3 0.6 reduce_sum.9
  176.0 0.0 slice-start.1
  176.0 9.2 %convert_element_type.3 = f32[3,2,1024,512]{3,2,1,0:T(8,128)} convert(bf16[3,2,1024,512]{3,2,1,0:T(8,128)(2,1)} %get-tuple-element.25) | non-fusion elementwise | flops 3145728 | bytes 18874368 | tf_op jit(solution)/shard_map/convert_element_type | solution.py:786
  185.2 2.3 %slice_bitcast_fusion = f32[512,512]{1,0:T(8,128)} fusion(f32[3,2,1024,512]{3,2,1,0:T(8,128)} %convert_element_type.3), kind=kLoop, calls=%fused_computation | loop fusion | bytes 2097152 | tf_op jit(solution)/shard_map/squeeze | solution.py:790
  187.5 0.0 slice-done
  187.5 0.0 slice-done.1
  187.5 3.4 %fusion = (f32[1,2,1024,512]{3,2,1,0:T(8,128)}, f32[1,2,1024,512]{3,2,1,0:T(8,128)S(1)}, f32[1,2,1024,512]{3,2,1,0:T(8,128)S(1)}) fusion(bf16[3,2,1024,512]{3,2,1,0:T(8,128)(2,1)S(1)} %bitcast.28), kind=kLoop, calls=%fused_computation.4 | loop fusion | bytes 25165824 | tf_op jit(solution)/shard_map/slice | solution.py:787
  190.8 2.5 %copy.46 = f32[4,64,8,512]{3,2,0,1:T(8,128)} copy(f32[4,64,8,512]{3,2,1,0:T(8,128)S(1)} %bitcast.29) | data formatting | bytes 8388608 | tf_op jit(solution)/shard_map/reshape | solution.py:788
  193.3 0.3 slice.73
  193.6 2.3 %copy.45 = f32[3,512,512]{1,2,0:T(8,128)} copy(f32[3,512,512]{2,1,0:T(8,128)S(1)} %slice.73) | data formatting | bytes 6291456
  195.9 0.0 copy-start.1
  195.9 0.0 copy-start
  195.9 3.7 %copy.44 = f32[512,1536]{1,0:T(8,128)} copy(f32[512,1536]{0,1:T(8,128)} %bitcast.31) | data formatting | bytes 6291456
  199.6 0.0 copy-done.1
  199.6 1.0 copy.50
  200.6 0.0 copy-done
  200.6 1.0 copy.51
  (1 shorter events, 0.0 us)
Async XLA Ops:
  169.5 18.0 %slice-start = ((s8[6291456]{0:T(1024)(128)(4,1)}), s8[2097152]{0:T(1024)(128)(4,1)S(1)}, s32[]{:S(2)}) async-start(s8[6291456]{0:T(1024)(128)(4,1)} %bitcast.27), calls=%async_computation | async-start | bytes 4194304
  176.0 11.5 %slice-start.1 = ((s8[6291456]{0:T(1024)(128)(4,1)}), s8[4194304]{0:T(1024)(128)(4,1)S(1)}, s32[]{:S(2)}) async-start(s8[6291456]{0:T(1024)(128)(4,1)} %bitcast.27), calls=%async_computation.1 | async-start | bytes 8388608
  195.9 3.7 %copy-start.1 = (bf16[4,1,256,512]{3,2,1,0:T(8,128)(2,1)S(1)}, bf16[4,1,256,512]{3,2,1,0:T(8,128)(2,1)}, u32[]{:S(2)}) copy-start(bf16[4,1,256,512]{3,2,1,0:T(8,128)(2,1)} %get-tuple-element.78) | copy-start | bytes 3145732
  195.9 4.7 %copy-start = (bf16[4,1,256,512]{3,2,1,0:T(8,128)(2,1)S(1)}, bf16[4,1,256,512]{3,2,1,0:T(8,128)(2,1)}, u32[]{:S(2)}) copy-start(bf16[4,1,256,512]{3,2,1,0:T(8,128)(2,1)} %get-tuple-element.79) | copy-start | bytes 3145732
where the time goes:
time: 202 us
  Pallas kernels  169 us (84%)
  local copies, waits for them, and re-layouts  22.2 us (11%)
  other arithmetic  9.87 us (5%)
    pallas_call x1, Pallas kernels, body(): pl.pallas_call(functools.partial(block_kernel, n_img, n_win), out_shape=(...  169 us
    unnamed x14, local copies, waits for them, and re-layouts  9.31 us
    convert_element_type x1, other arithmetic, body(): sums = sums.astype(F32)  9.24 us

commit v1 on v0

v1 whole, which is shorter than its diff:
```python
import functools

import jax
import jax.numpy as jnp
import numpy as np
from jax import lax
from jax.experimental import pallas as pl
from jax.experimental.pallas import tpu as pltpu
from jax.sharding import PartitionSpec as P

WIN = 16
TOK = WIN * WIN
EPS_DIR = 1e-06
EPS_NORM = 1e-05
MASK_FILL = -100.0
BIAS_RANGE = 16.0
INV_ROOT_TWO = 0.7071067811865476
INV_ROOT_TWOPI = 0.3989422804014327
LOG2_E = 1.4426950408889634
MESH = pl.DeviceIdType.MESH
BF = jnp.bfloat16
F32 = jnp.float32

(ROW_QB, ROW_VB, ROW_LS, ROW_W1, ROW_B1, ROW_W2, ROW_BP, ROW_G1, ROW_S1, ROW_B2, ROW_G2, ROW_S2,
 ROW_BE, SMALL_ROWS) = (0, 1, 2, 3, 5, 6, 22, 23, 24, 25, 26, 27, 28, 32)

SCHEDULE = {
    "a1": ((0, 0),),
    "a3": ((1, 0), (0, 1)),
    "d0": ((1, 1),),
    "d1": ((0, 2),),
    "d2": ((1, 2),),
    "d3": ((0, 3),),
    "b0": ((1, 3),),
    "b1": ((2, 0),),
    "b3": ((3, 0), (2, 1)),
    "gproj": ((4, 0), (3, 1), (0, 4), (4, 1)),
    "r0": ((1, 4), (2, 2), (3, 2), (0, 5)),
    "r1": ((4, 2), (2, 3), (1, 5), (3, 3)),
    "r2": ((0, 6), (4, 3), (1, 6), (2, 4)),
    "r3": ((3, 4), (0, 7)),
    "gq0": ((5, 0), (4, 4), (0, 8), (1, 7), (5, 1)),
    "r4": ((1, 8), (2, 5)),
    "r5": ((3, 5), (4, 5), (5, 2), (2, 6)),
    "r6": ((3, 6), (4, 6), (5, 3)),
    "r7": ((2, 7),),
    "gq1": ((6, 0), (5, 4), (3, 7), (2, 8), (6, 1), (4, 7), (3, 8), (4, 8)),
    "bb": ((5, 5),),
    "net": ((7, 0), (5, 6), (6, 2), (7, 1)),
    "end": ((6, 3), (6, 4), (7, 2), (6, 5), (7, 3), (6, 6), (7, 4)),
}


def nn(a, b):
    return lax.dot_general(a, b, (((1,), (0,)), ((), ())), preferred_element_type=F32)


def nt(a, b):
    return lax.dot_general(a, b, (((1,), (1,)), ((), ())), preferred_element_type=F32)


def tn(a, b):
    return lax.dot_general(a, b, (((0,), (0,)), ((), ())), preferred_element_type=F32)


def split3(v):
    hi = v.astype(BF)
    rest = v - hi.astype(F32)
    mid = rest.astype(BF)
    return hi, mid, (rest - mid.astype(F32)).astype(BF)


def gelu_parts(v):
    cap = 0.5 + 0.5 * lax.erf(v * INV_ROOT_TWO)
    return cap, INV_ROOT_TWOPI * jnp.exp2(v * v * (-0.5 * LOG2_E))


def col_sum(v):
    return jnp.sum(v.reshape(v.shape[0] // 8, 8, v.shape[1]), axis=0)


def to_blocks(v):
    n = v.shape[-1]
    t = v.reshape(2, 8, 2, 8, n)
    return [[t[qr, :, qc].reshape(64, n) for qc in range(2)] for qr in range(2)]


def from_blocks(quads):
    n = quads[0][0].shape[-1]
    rows = []
    for qr in range(2):
        a = quads[qr][0].reshape(8, 1, 8, n)
        b = quads[qr][1].reshape(8, 1, 8, n)
        rows.append(jnp.concatenate([a, b], axis=1).reshape(128, n))
    return jnp.concatenate(rows, axis=0)


def one_hot_places(c):
    l = lax.broadcasted_iota(jnp.int32, (256, 512), 0)
    k = lax.broadcasted_iota(jnp.int32, (256, 512), 1) + 512 * c
    return jnp.where(l == 8 * (15 - k // 128) + k % 128, 1.0, 0.0).astype(BF)


def one_hot_pick():
    k = lax.broadcasted_iota(jnp.int32, (1024, 256), 0)
    l = lax.broadcasted_iota(jnp.int32, (1024, 256), 1)
    return jnp.where(k == 32 * (l // 8) + l % 8, 1.0, 0.0).astype(BF)


def table_coords():
    k = np.arange(1024)
    out = np.zeros((2, 1024), np.float64)
    for i, off in enumerate((15 - k // 32, 15 - k % 32)):
        u = off * (8.0 / 15.0)
        out[i] = np.sign(u) * np.log2(np.abs(u) + 1.0) / 3.0
    rows = np.zeros((8, 1024), np.float32)
    rows[0:2] = out
    rows[2] = 1.0
    cols = np.zeros((1024, 8), np.float32)
    cols[:, 0:2] = out.T
    return rows, cols


def net_first(cols, w1, b1):
    return cols[:, 0:1] * w1[0:1, :] + cols[:, 1:2] * w1[1:2, :] + b1


def block_kernel(
    n_img, n_win,
    x_hbm, cot_hbm, wqkv_hbm, wproj_hbm, we_hbm, wc_hbm, qb, vb, hls, w1, b1, w2t, bproj, g1, s1, be, bc, g2, s2,
    crow, ccol,
    res_hbm, gin_hbm, wide_hbm, qkv_hbm, small_out,
    xr, cr, xroll, bias, ex, qs, kl, vl, qinv, kinv, isum, mixed, mixlo, blk, dmid, act, dhid, dout,
    mlow, slope, tab, part, acc_s, asum, rec, far, wqkv, wproj, we, wc,
    small_s, small_c, small_p, small_z, small_far, small_o,
    s_x, r_x, s_c, r_c, s_res, r_res, s_gin, r_gin, s_ar, r_ar, l_ar, s_sm, r_sm, s_w,
):
    img = lax.axis_index("img")
    me = lax.axis_index("win")
    extra = n_img // 8
    core = lax.rem(me, 2)
    ypos = me // 2
    xpos = lax.rem(img, 2)
    zpos = lax.rem(img // 2, 4)
    upper = img // 8

    def ring_to(k):
        return (img, lax.rem(me + k, n_win))

    def ring_from(k):
        return lax.rem(me + n_win - k, n_win)

    core_peer = (img, me + 1 - 2 * core)
    y_peer = (img, lax.rem(me + 2, 4))
    x_peer = (img + 1 - 2 * xpos, me)
    plane_pos = 2 * xpos + ypos

    def z_peer(k):
        return (upper * 8 + lax.rem(zpos + k, 4) * 2 + xpos, me)

    def plane_peer(k):
        to = lax.rem(plane_pos + k, 4)
        return (img + to // 2 - xpos, lax.rem(to, 2) * 2 + core)

    def far_peer(k):
        return (lax.rem(upper + k, extra) * 8 + zpos * 2 + xpos, me)

    weights = [
        pltpu.make_async_copy(a, b, s_w.at[i])
        for i, (a, b) in enumerate(((wqkv_hbm, wqkv), (wproj_hbm, wproj), (we_hbm, we), (wc_hbm, wc)))
    ]

    barrier = pltpu.get_barrier_semaphore()
    others = [ring_to(k) for k in range(1, n_win)] + [x_peer, (img + 1 - 2 * xpos, lax.rem(me + 2, 4))]
    others += [z_peer(k) for k in range(1, 4)] + [far_peer(k) for k in range(1, extra)]
    for peer in others:
        pl.semaphore_signal(barrier, inc=1, device_id=peer, device_id_type=MESH)
    pl.semaphore_wait(barrier, len(others))

    def remote(src, dst, ssem, rsem, peer):
        return pltpu.make_async_remote_copy(
            src_ref=src, dst_ref=dst, send_sem=ssem, recv_sem=rsem, device_id=peer, device_id_type=MESH
        )

    def spread(src_hbm, dst, ssem, rsem, k):
        to = lax.rem(me + k, n_win)
        return remote(src_hbm.at[to, 0], dst.at[me], ssem.at[k], rsem.at[k], ring_to(k))

    def spread_in(src_hbm, dst, ssem, rsem, k):
        frm = ring_from(k)
        return remote(src_hbm.at[frm, 0], dst.at[frm], ssem.at[k], rsem.at[k], ring_to(k))

    def own_part(src_hbm, dst, sem):
        return pltpu.make_async_copy(src_hbm.at[me, 0], dst.at[me], sem.at[0])

    def half_rows(w, half):
        return pl.ds(pl.multiple_of(128 * (1 - w // 2 if half == 0 else w // 2), 128), 128)

    def x_send(k, half):
        to, rows = lax.rem(me + k, n_win), half_rows(me, half)
        return remote(
            x_hbm.at[to, 0, rows], xr.at[me, rows], s_x.at[half, k], r_x.at[half, k], ring_to(k)
        )

    def x_arrival(k, half):
        frm = ring_from(k)
        rows = half_rows(frm, half)
        return remote(x_hbm.at[frm, 0, rows], xr.at[frm, rows], s_x.at[half, k], r_x.at[half, k], ring_to(k))

    for half in range(2):
        for k in (2, 1, 3):
            x_send(k, half).start()
    own_x = own_part(x_hbm, xr, r_x.at[0])
    own_x.start()
    for c in weights:
        c.start()

    def net_piece(c):
        rows = pl.ds(pl.multiple_of(256 * c, 256), 256)
        return rows, net_first(ccol[rows, :], w1[...], b1[...][None, :])

    def look_up(c, _):
        cols, pre = net_piece(c)
        logits = lax.dot_general(
            w2t[...], pre * gelu_parts(pre)[0], (((1,), (1,)), ((), ())),
            precision=lax.Precision.HIGHEST, preferred_element_type=F32,
        )
        tab[:, cols] = BIAS_RANGE / (1.0 + jnp.exp(-logits))
        return 0

    lax.fori_loop(0, 4, look_up, 0)
    for u in range(24):
        part[:, u, :] = pltpu.roll(tab[...], 1001 + u, 1)
    pick = one_hot_pick()
    short = jnp.concatenate(
        [sum(nn(p, pick) for p in split3(part[4 * i : 4 * i + 4].reshape(96, 1024))) for i in range(4)], axis=0
    )
    short_parts = split3(short)
    for c in range(4):
        places = one_hot_places(c)
        wide = sum(nn(p, places) for p in short_parts)
        for r in range(4):
            row = 8 * (4 * c + r)
            bias[:, :, row : row + 8, :] = wide[:, 128 * r : 128 * r + 128].reshape(16, 3, 8, 128)

    lane = lax.broadcasted_iota(jnp.int32, (1, 128), 1)
    head_mask = [jnp.where(lane // 32 == hh, 1.0, 0.0).astype(BF) for hh in range(4)]
    l0 = lax.broadcasted_iota(jnp.int32, (256, 256), 0)
    l1 = lax.broadcasted_iota(jnp.int32, (256, 256), 1)
    head_ones = jnp.where(l0 // 32 == l1 // 32, 1.0, 0.0).astype(BF)

    def scale_lanes(p):
        wide = lax.broadcasted_iota(jnp.int32, (1, 256), 1) // 32
        out = jnp.zeros((1, 256), F32)
        for i in range(8):
            out = jnp.where(wide == i, hls[8 * p + i], out)
        return jnp.exp(out)

    def lay(half):
        def one(w, _):
            late = w // 2 if half == 0 else 1 - w // 2
            rows = pl.ds(pl.multiple_of(128 * (1 - late), 128), 128)
            v = xr[w, rows, :].astype(F32).reshape(8, 2, 8, 512)
            for qc in range(2):
                bcol = 1 - qc
                ocol = lax.rem(w, 2) if bcol == 0 else 1 - lax.rem(w, 2)
                at = pl.ds(pl.multiple_of((bcol * 2 + late) * 64, 64), 64)
                xroll[2 * half + ocol, at, :] = v[:, qc].reshape(64, 512).astype(BF)
            return 0

        lax.fori_loop(0, 4, one, 0)

    own_x.wait()
    for k in (1, 2, 3):
        x_arrival(k, 0).wait_recv()
    lay(0)
    weights[0].wait()
    weights[1].wait()

    row_half = lax.broadcasted_iota(jnp.int32, (128, 128), 0) // 64
    col_half = lax.broadcasted_iota(jnp.int32, (128, 128), 1) // 64
    apart = jnp.where(row_half == col_half, 0.0, MASK_FILL)

    def home(o, bcol, br):
        return lax.rem(2 * (o // 2) + br + 1, 4), lax.rem(2 * lax.rem(o, 2) + bcol + 1, 4)

    def attend(o, _):
        @pl.when(o == 2)
        def _():
            for k in (1, 2, 3):
                x_arrival(k, 1).wait_recv()
            for k in (2, 1, 3):
                spread(cot_hbm, cr, s_c, r_c, k).start()
            own_part(cot_hbm, cr, r_c).start()
            lay(1)

        xw = xroll[o]
        for p in range(2):
            cols = slice(256 * p, 256 * p + 256)
            q = nn(xw, wqkv[:, cols]) + qb[cols][None, :]
            qi = lax.rsqrt(nn((q * q).astype(BF), head_ones) + EPS_DIR)
            qsc = (q * qi * scale_lanes(p)).astype(BF)
            k = nn(xw, wqkv[:, 512 + 256 * p : 768 + 256 * p])
            ki = lax.rsqrt(nn((k * k).astype(BF), head_ones) + EPS_DIR)
            kn = (k * ki).astype(BF)
            v = (nn(xw, wqkv[:, 1024 + 256 * p : 1280 + 256 * p]) + vb[cols][None, :]).astype(BF)
            for i in range(2):
                half = slice(128 * i, 128 * i + 128)
                qs[o, 2 * p + i] = qsc[:, half]
                kl[o, 2 * p + i] = kn[:, half]
                vl[o, 2 * p + i] = v[:, half]
                qinv[o, 2 * p + i] = qi[:, half].astype(BF)
                kinv[o, 2 * p + i] = ki[:, half].astype(BF)
        rows_cut = jnp.where(o // 2 == 1, apart, 0.0)
        cols_cut = jnp.where(lax.rem(o, 2) == 1, jnp.full((128, 128), MASK_FILL, F32), rows_cut)

        for g in range(4):
            qg, kg, vg = qs[o, g], kl[o, g], vl[o, g]
            sc = nt(jnp.concatenate([qg * mask for mask in head_mask], axis=0), kg)
            for hh in range(4):
                h, n = 4 * g + hh, 256 * hh
                ex[o, g, hh, 0:128, 0:128] = jnp.exp(sc[n : n + 128, 0:128] + bias[h, 1] + rows_cut).astype(BF)
                ex[o, g, hh, 0:128, 128:256] = jnp.exp(sc[n : n + 128, 128:256] + bias[h, 0] + cols_cut).astype(BF)
                ex[o, g, hh, 128:256, 0:128] = jnp.exp(sc[n + 128 : n + 256, 0:128] + bias[h, 2] + cols_cut).astype(BF)
                ex[o, g, hh, 128:256, 128:256] = jnp.exp(
                    sc[n + 128 : n + 256, 128:256] + bias[h, 1] + rows_cut
                ).astype(BF)
            ones = [jnp.broadcast_to(mask, (256, 128)) for mask in head_mask]
            total = nn(
                jnp.concatenate([ex[o, g, hh] for hh in range(4)], axis=1),
                jnp.concatenate(
                    [jnp.concatenate([vg * mask, one], axis=1) for mask, one in zip(head_mask, ones)], axis=0
                ),
            )
            inv = 1.0 / total[:, 128:256]
            isum[o, g] = inv
            mix = total[:, 0:128] * inv
            mix_hi = mix.astype(BF)
            mixed[o, :, 128 * g : 128 * g + 128] = mix_hi
            mixlo[o, :, 128 * g : 128 * g + 128] = (mix - mix_hi.astype(F32)).astype(BF)

        branch = (nn(mixed[o], wproj[...]) + bproj[...][None, :]).astype(BF)
        for bcol in range(2):
            for br in range(2):
                at = (bcol * 2 + br) * 64
                brow, bc_ = home(o, bcol, br)
                blk[brow, bc_] = branch[at : at + 64, :]
        return 0

    lax.fori_loop(0, 4, attend, 0)

    for k in (0, 1, 2, 3):
        if k == 0:
            own_part(cot_hbm, cr, r_c).wait()
        else:
            spread_in(cot_hbm, cr, s_c, r_c, k).wait_recv()
    weights[2].wait()
    weights[3].wait()
    acc_s[...] = jnp.zeros_like(acc_s)

    def res_copy(w):
        return remote(xr.at[w], res_hbm.at[me, 0], s_res.at[w], r_res.at[me], (img, w))

    def flat(quads):
        return jnp.concatenate([quads[0][0], quads[0][1], quads[1][0], quads[1][1]], axis=0)

    def first_norm(w):
        wr, wcol = w // 2, lax.rem(w, 2)
        back = jnp.concatenate(
            [blk[2 * wr + qr, 2 * wcol + qc] for qr in range(2) for qc in range(2)], axis=0
        ).astype(F32)
        ctr = back - jnp.mean(back, axis=1, keepdims=True)
        r1 = lax.rsqrt(jnp.mean(ctr * ctr, axis=1, keepdims=True) + EPS_NORM)
        return ctr * r1, r1

    def dense(w, _):
        e = flat(to_blocks(cr[w].astype(F32)))
        z1, _ = first_norm(w)
        middle = flat(to_blocks(xr[w].astype(F32))) + z1 * g1[...][None, :] + s1[...][None, :]
        ml = middle.astype(BF)
        rows = pl.ds(pl.multiple_of(w * TOK, TOK), TOK)
        mlow[rows, :] = ml
        out = jnp.zeros((TOK, 512), F32)
        for c in range(4):
            cols = slice(512 * c, 512 * c + 512)
            hid = nn(ml, we[:, cols]) + be[cols][None, :]
            cap, low = gelu_parts(hid)
            a = (hid * cap).astype(BF)
            act[c, rows, :] = a
            dhid[c, rows, :] = (cap + hid * low).astype(BF)
            out = out + nn(a, wc[cols, :])
        out = out + bc[...][None, :]
        ctr2 = out - jnp.mean(out, axis=1, keepdims=True)
        r2 = lax.rsqrt(jnp.mean(ctr2 * ctr2, axis=1, keepdims=True) + EPS_NORM)
        z2 = ctr2 * r2
        result = middle + z2 * g2[...][None, :] + s2[...][None, :]
        quads = [[result[128 * qr + 64 * qc : 128 * qr + 64 * qc + 64] for qc in range(2)] for qr in range(2)]
        xr[w] = from_blocks(quads).astype(BF)

        @pl.when(w != me)
        def _():
            res_copy(w).start()

        acc_s[0] += col_sum(e * z2)
        acc_s[1] += col_sum(e)
        dn = e * g2[...][None, :]
        dv = r2 * (
            dn - jnp.mean(dn, axis=1, keepdims=True) - z2 * jnp.mean(dn * z2, axis=1, keepdims=True)
        )
        do = dv.astype(BF)
        dout[rows, :] = do
        acc_s[2] += col_sum(do.astype(F32))
        return 0

    lax.fori_loop(0, 4, dense, 0)
    own_res = pltpu.make_async_copy(xr.at[me], res_hbm.at[me, 0], r_res.at[me])
    own_res.start()

    digits = {"x": (xpos, 2), "y": (ypos, 2), "z": (zpos, 4), "p": (plane_pos, 4)}

    def digit_peer(d, k):
        if d == "z":
            return z_peer(k)
        if d == "p":
            return plane_peer(k)
        return x_peer if d == "x" else y_peer

    def sum_unit(a, src, land, out, order):
        n = src.shape[1]
        levels, at, size, room, sem = [], core * 256, 256, 256, 1
        for d in order:
            pos, count = digits[d]
            part_size = size // count
            levels.append((d, pos, count, at, part_size, room, sem))
            at, room, sem = at + pos * part_size, room + (count - 1) * part_size, sem + count - 1
            size = part_size
        own_at, last = at, len(order) - 1

        def rows(start, length):
            return pl.ds(pl.multiple_of(start, 16), length)

        def copy(src_at, dst, length, i, peer):
            return remote(src.at[rows(src_at, length)], dst, s_ar.at[a, i], r_ar.at[a, i], peer)

        def core_send():
            return copy((1 - core) * 256, land.at[pl.ds(0, 256)], 256, 0, core_peer)

        def down(j, k):
            d, pos, count, at, length, room, sem = levels[j]
            dst = land.at[pl.ds(room + (k - 1) * length, length)]
            return copy(at + lax.rem(pos + k, count) * length, dst, length, sem + k - 1, digit_peer(d, k))

        def up(j, k, pos):
            d, _, count, at, length, _, sem = levels[j]
            here = out.at[rows(at + pos * length, length)]
            from_ = src.at[rows(own_at, length)] if j == last else here
            return remote(from_, here, s_ar.at[a, 6 + sem + k], r_ar.at[a, 6 + sem + k], digit_peer(d, k))

        def core_up(c):
            here = out.at[rows(c * 256, 256)]
            return remote(here, here, s_ar.at[a, 14], r_ar.at[a, 14], core_peer)

        def far_send(k):
            return copy(own_at, far.at[a, k - 1, :, 0:n], 16, 15 + k - 1, far_peer(k))

        def peers(j):
            return range(1, levels[j][2])

        def from_pos(j, k):
            return lax.rem(levels[j][1] + levels[j][2] - k, levels[j][2])

        def local():
            here = rows(own_at, 16)
            return pltpu.make_async_copy(src.at[here], out.at[here], l_ar.at[a])

        def step_core():
            core_send().start()

        def step_down(j):
            if j == 0:
                core_send().wait_recv()
                at = rows(core * 256, 256)
                src[at, :] = src[at, :] + land[0:256, :]
            else:
                take(j - 1)
            for k in peers(j):
                down(j, k).start()

        def take(j):
            d, pos, count, at, length, room, sem = levels[j]
            here = rows(at + pos * length, length)
            for k in peers(j):
                down(j, k).wait_recv()
            total = src[here, :].astype(F32)
            for k in peers(j):
                r = room + (k - 1) * length
                total = total + land[r : r + length, :].astype(F32)
            src[here, :] = total.astype(BF)

        def step_turn():
            take(last)
            if extra > 1:
                here = rows(own_at, 16)
                for k in range(1, extra):
                    far_send(k).start()
                total = src[here, :].astype(F32)
                for k in range(1, extra):
                    far_send(k).wait()
                    total = total + far[a, k - 1, :, 0:n].astype(F32)
                src[here, :] = total.astype(BF)
            for k in peers(last):
                up(last, k, levels[last][1]).start()
            local().start()

        def step_up(j):
            if j == last:
                local().wait()
            for k in peers(j):
                up(j, k, from_pos(j, k)).wait_recv()
            if j == 0:
                core_up(core).start()
            else:
                for k in peers(j - 1):
                    up(j - 1, k, levels[j - 1][1]).start()

        def step_last():
            core_up(1 - core).wait_recv()

        def step_sent():
            core_send().wait_send()
            core_up(core).wait_send()
            for j in range(last + 1):
                for k in peers(j):
                    down(j, k).wait_send()
                    up(j, k, levels[j][1]).wait_send()

        steps = [step_core] + [functools.partial(step_down, j) for j in range(last + 1)] + [step_turn]
        return steps + [functools.partial(step_up, j) for j in range(last, -1, -1)] + [step_last, step_sent]

    def together(units):
        return [lambda steps=steps: [step() for step in steps] for steps in zip(*units)]

    orders = ("xyz", "yxz")
    wide_units = [sum_unit(a, asum.at[a], rec.at[a], wide_hbm.at[a], orders[a % 2]) for a in range(9)]
    groups = [together(wide_units[2 * i : 2 * i + 2]) for i in range(4)] + [wide_units[8]]
    for p in range(2):
        part_units = []
        for i in range(3):
            place = (pl.ds(512 * (i // 2), 512), pl.ds(256 * (i % 2), 256))
            part_units.append(
                sum_unit(
                    9 + 3 * p + i, act.at[p].at[place], act.at[2 + p].at[place], qkv_hbm.at[p, i],
                    "pz",
                )
            )
        groups.append(together(part_units))

    def small_steps():
        mine, other = pl.ds(pl.multiple_of(16 * core, 16), 16), pl.ds(pl.multiple_of(16 - 16 * core, 16), 16)

        def copy(src, dst, i, peer):
            return remote(src, dst, s_sm.at[i], r_sm.at[i], peer)

        def core_send():
            return copy(small_s.at[0, other], small_c, 0, core_peer)

        def plane_send(k):
            return copy(small_s.at[1, mine], small_p.at[k - 1], k, plane_peer(k))

        def z_send(k):
            return copy(small_s.at[2, mine], small_z.at[k - 1], 3 + k, z_peer(k))

        def far_copy(k):
            return copy(small_s.at[3, mine], small_far.at[k - 1], 7 + k, far_peer(k))

        def core_up(rows):
            return copy(small_o.at[rows], small_o.at[rows], 7, core_peer)

        def step0():
            core_send().start()

        def step1():
            core_send().wait_recv()
            small_s[1, mine, :] = small_s[0, mine, :] + small_c[...]
            for k in range(1, 4):
                plane_send(k).start()

        def step2():
            total = small_s[1, mine, :]
            for k in range(1, 4):
                plane_send(k).wait_recv()
                total = total + small_p[k - 1]
            small_s[2, mine, :] = total
            for k in range(1, 4):
                z_send(k).start()

        def step3():
            total = small_s[2, mine, :]
            for k in range(1, 4):
                z_send(k).wait_recv()
                total = total + small_z[k - 1]
            if extra > 1:
                small_s[3, mine, :] = total
                for k in range(1, extra):
                    far_copy(k).start()
                for k in range(1, extra):
                    far_copy(k).wait()
                    total = total + small_far[k - 1]
            small_o[mine, :] = total
            core_up(mine).start()

        def step4():
            core_up(other).wait_recv()
            small_out[...] = small_o[...]

        def step5():
            core_send().wait_send()
            core_up(mine).wait_send()
            for k in range(1, 4):
                plane_send(k).wait_send()
                z_send(k).wait_send()

        return [step0, step1, step2, step3, step4, step5]

    groups.append(small_steps())

    def run(name):
        for at, j in SCHEDULE.get(name, ()):
            groups[at][j]()

    def run_in(prefix, i):
        for at in range(8):
            if SCHEDULE.get(f"{prefix}{at}"):

                @pl.when(i == at)
                def _(at=at):
                    run(f"{prefix}{at}")

    for c in range(4):
        asum[c] = tn(act[c], dout[...]).astype(BF)
        run(f"a{c}")

    def dense_back(w, _):
        wr, wcol = w // 2, lax.rem(w, 2)
        rows = pl.ds(pl.multiple_of(w * TOK, TOK), TOK)
        do = dout[rows, :]
        dm = flat(to_blocks(cr[w].astype(F32)))
        for c in range(4):
            cols = slice(512 * c, 512 * c + 512)
            dh = (nt(do, wc[cols, :]) * dhid[c, rows, :].astype(F32)).astype(BF)
            dhid[c, rows, :] = dh
            acc_s[3 + c] += col_sum(dh.astype(F32))
            dm = dm + nt(dh, we[:, cols])
        z1, r1 = first_norm(w)
        acc_s[7] += col_sum(dm * z1)
        acc_s[8] += col_sum(dm)
        dn1 = dm * g1[...][None, :]
        db = r1 * (
            dn1 - jnp.mean(dn1, axis=1, keepdims=True) - z1 * jnp.mean(dn1 * z1, axis=1, keepdims=True)
        )
        db = db.astype(BF)
        for qr in range(2):
            for qc in range(2):
                at = 128 * qr + 64 * qc
                dmid[2 * wr + qr, 2 * wcol + qc] = dm[at : at + 64]
                blk[2 * wr + qr, 2 * wcol + qc] = db[at : at + 64]
        run_in("d", w)
        return 0

    lax.fori_loop(0, 4, dense_back, 0)
    for c in range(4):
        asum[4 + c] = tn(mlow[...], dhid[c]).astype(BF)
        run(f"b{c}")

    bias[...] = jnp.zeros_like(bias)

    def gather(o, _):
        for bcol in range(2):
            for br in range(2):
                at = (bcol * 2 + br) * 64
                brow, bc_ = home(o, bcol, br)
                cr[o, at : at + 64, :] = blk[brow, bc_]
        return 0

    lax.fori_loop(0, 4, gather, 0)
    asum[8] = tn(mixed[...].reshape(1024, 512), cr[...].reshape(1024, 512)).astype(BF)
    run("gproj")
    head_ones_half = head_ones[0:128, 0:128]
    minus = jnp.full((256, 128), -1.0, BF)
    lane32 = lax.rem(lax.broadcasted_iota(jnp.int32, (256, 128), 1), 32)

    def retreat(it, _):
        p, o = it // 4, lax.rem(it, 4)
        half = pl.ds(pl.multiple_of(256 * p, 256), 256)
        dmx = nt(cr[o], wproj[half, :])
        rows = pl.ds(pl.multiple_of(o * TOK, TOK), TOK)
        scales = scale_lanes(p)
        for gi in range(2):
            g = 2 * p + gi
            lanes = pl.ds(pl.multiple_of(128 * g, 128), 128)
            qg, kg, vg = qs[o, g], kl[o, g], vl[o, g]
            dmg = dmx[:, 128 * gi : 128 * gi + 128] * isum[o, g]
            dmp = dmg.astype(BF)
            mix = mixed[o, :, lanes].astype(F32) + mixlo[o, :, lanes].astype(F32)
            prod = dmp.astype(F32) * mix
            delta = sum(nn(p, head_ones_half) for p in split3(prod)[:2])
            delta_hi, delta_lo, _ = split3(delta)
            prod = jnp.where(lane32 == 0, delta_hi, jnp.where(lane32 == 1, delta_lo, jnp.zeros_like(delta_lo)))
            vw = jnp.concatenate([vg, minus], axis=1)
            dmp4 = jnp.concatenate([dmp * mask for mask in head_mask], axis=0)
            left = jnp.concatenate([dmp4, jnp.concatenate([prod * mask for mask in head_mask], axis=0)], axis=1)
            e4 = ex[o, g].reshape(1024, 256)
            dsf = nt(left, vw) * e4.astype(F32)
            ds = dsf.astype(BF)
            for hh in range(4):
                h, n = 4 * g + hh, 256 * hh
                bias[h, 1] += dsf[n : n + 128, 0:128] + dsf[n + 128 : n + 256, 128:256]
                bias[h, 0] += dsf[n : n + 128, 128:256]
                bias[h, 2] += dsf[n + 128 : n + 256, 0:128]
            dq = nn(
                jnp.concatenate([ds[256 * hh : 256 * hh + 256] for hh in range(4)], axis=1),
                jnp.concatenate([kg * mask for mask in head_mask], axis=0),
            )
            dk = tn(ds, jnp.concatenate([qg * mask for mask in head_mask], axis=0))
            dv = tn(e4, dmp4)
            qf, kf = qg.astype(F32), kg.astype(F32)
            scale = scales[:, 128 * gi : 128 * gi + 128]
            tq = dq * qf
            acc_s[9, :, lanes] += col_sum(tq)
            aq = nn(tq.astype(BF), head_ones_half)
            ak = nn((dk * kf).astype(BF), head_ones_half)
            dhid[0, rows, lanes] = (qinv[o, g].astype(F32) * (scale * dq - (1.0 / scale) * qf * aq)).astype(BF)
            dhid[1, rows, lanes] = (kinv[o, g].astype(F32) * (dk - kf * ak)).astype(BF)
            dhid[2, rows, lanes] = dv.astype(BF)
        moved = sum(
            nt(dhid[i, rows, half], wqkv[:, pl.ds(pl.multiple_of(512 * i + 256 * p, 256), 256)])
            for i in range(3)
        )
        for bcol in range(2):
            for br in range(2):
                at = (bcol * 2 + br) * 64
                brow, bc_ = home(o, bcol, br)
                dmid[brow, bc_] += moved[at : at + 64, :]
        run_in("r", it)

        @pl.when(lax.rem(it, 4) == 3)
        def _():
            xflat = xroll[...].reshape(1024, 512)
            for i in range(3):
                grad = tn(xflat, dhid[i, :, half]).astype(BF)
                act[p, 512 * (i // 2) : 512 * (i // 2) + 512, 256 * (i % 2) : 256 * (i % 2) + 256] = grad

        run_in("gq", jnp.where(lax.rem(it, 4) == 3, p, -1))
        return 0

    lax.fori_loop(0, 8, retreat, 0)

    def gin_copy(w):
        return remote(slope.at[w], gin_hbm.at[me, 0], s_gin.at[w], r_gin.at[me], (img, w))

    def finish(w, _):
        wr, wcol = w // 2, lax.rem(w, 2)
        quads = [[dmid[2 * wr + qr, 2 * wcol + qc] for qc in range(2)] for qr in range(2)]
        slope[w] = from_blocks(quads).astype(BF)

        @pl.when(w != me)
        def _():
            gin_copy(w).start()

        return 0

    lax.fori_loop(0, 4, finish, 0)
    own_gin = pltpu.make_async_copy(slope.at[me], gin_hbm.at[me, 0], r_gin.at[me])
    own_gin.start()
    run("finish")

    row_ones = jnp.ones((8, 1024), BF)

    def put(row, v):
        small_s[0, row : row + v.shape[0], :] = v

    put(ROW_QB, nn(row_ones, dhid[0])[0:1])
    put(ROW_VB, nn(row_ones, dhid[2])[0:1])
    put(ROW_BP, nn(row_ones, cr[...].reshape(1024, 512))[0:1])
    for row, i in ((ROW_LS, 9), (ROW_G1, 7), (ROW_S1, 8), (ROW_B2, 2), (ROW_G2, 0), (ROW_S2, 1)):
        put(row, jnp.sum(acc_s[i], axis=0, keepdims=True))
    for c in range(4):
        put(ROW_BE + c, jnp.sum(acc_s[3 + c], axis=0, keepdims=True))
    run("puts")
    short = jnp.zeros((384, 256), F32)
    for c in range(4):
        places = one_hot_places(c)
        left = jnp.concatenate(
            [bias[:, :, 8 * r : 8 * r + 8, :].reshape(384, 128) for r in range(4 * c, 4 * c + 4)], axis=1
        )
        for p in split3(left)[:2]:
            short = short + nt(p, places)
    pick = one_hot_pick()
    for i in range(4):
        piece = split3(short[96 * i : 96 * i + 96])[:2]
        part[4 * i : 4 * i + 4] = sum(nt(p, pick) for p in piece).reshape(4, 24, 1024)
    run("bb")
    dtab = jnp.zeros((16, 1024), F32)
    for u in range(24):
        dtab = dtab + pltpu.roll(part[:, u, :], 23 - u, 1)
    tab[...] = dtab * tab[...] * (1.0 - tab[...] * (1.0 / BIAS_RANGE))
    small_s[0, ROW_W1 : ROW_W2 + 16, :] = jnp.zeros((ROW_W2 + 16 - ROW_W1, 512), F32)

    def net_back(c, _):
        cols, pre = net_piece(c)
        cap, low = gelu_parts(pre)
        dlog, dlog_lo, _ = split3(tab[:, cols])
        units, units_lo, _ = split3(pre * cap)
        small_s[0, ROW_W2 : ROW_W2 + 16, :] += nn(dlog, units) + nn(dlog_lo, units) + nn(dlog, units_lo)
        w_hi, w_lo, _ = split3(w2t[...])
        back = tn(dlog, w_hi) + tn(dlog_lo, w_hi) + tn(dlog, w_lo)
        dpre, dpre_lo, _ = split3(back * (cap + pre * low))
        hi, mid, _ = split3(crow[:, cols])
        net = nn(hi, dpre) + nn(mid, dpre) + nn(hi, dpre_lo)
        small_s[0, ROW_W1 : ROW_W1 + 3, :] += net[0:3]
        return 0

    lax.fori_loop(0, 4, net_back, 0)
    run("net")
    run("end")

    for group in groups:
        group[-1]()
    own_res.wait()
    own_gin.wait()
    for k in (1, 2, 3):
        frm, to = ring_from(k), lax.rem(me + k, n_win)
        x_send(k, 0).wait_send()
        x_send(k, 1).wait_send()
        spread(cot_hbm, cr, s_c, r_c, k).wait_send()
        res_copy(to).wait_send()
        gin_copy(to).wait_send()
        remote(xr.at[frm], res_hbm.at[frm, 0], s_res.at[frm], r_res.at[frm], (img, frm)).wait_recv()
        remote(slope.at[frm], gin_hbm.at[frm, 0], s_gin.at[frm], r_gin.at[frm], (img, frm)).wait_recv()


def widen_kernel(
    res, gin, wide, qkv, small,
    res_out, gin_out, w_qkv, g_qb, g_vb, g_ls, g_w1, g_b1, g_w2, w_proj, g_bp, g_g1, g_s1, w_fc1, g_be,
    w_fc2, g_b2, g_g2, g_s2,
    blocks, wide_in, qkv_in, wide_f, qkv_f, s_in, s_out, s_blocks,
):
    taken = [pltpu.make_async_copy(a, blocks.at[i], s_blocks.at[i]) for i, a in enumerate((res, gin))]
    passed = [pltpu.make_async_copy(blocks.at[i], a, s_blocks.at[2 + i]) for i, a in enumerate((res_out, gin_out))]
    pieces = []
    for i in range(9):
        if i < 4:
            place = w_fc2.at[pl.ds(512 * i, 512), :]
        elif i < 8:
            place = w_fc1.at[:, pl.ds(512 * (i - 4), 512)]
        else:
            place = w_proj
        pieces.append((wide.at[i], wide_in.at[i], wide_f.at[i], place))
    for i in range(6):
        place = w_qkv.at[:, pl.ds(512 * (i % 3) + 256 * (i // 3), 256)]
        pieces.append((qkv.at[i // 3, i % 3], qkv_in.at[i], qkv_f.at[i], place))
    loads = [pltpu.make_async_copy(a, b, s_in.at[i]) for i, (a, b, _, _) in enumerate(pieces)]
    stores = [pltpu.make_async_copy(c, d, s_out.at[i]) for i, (_, _, c, d) in enumerate(pieces)]
    for c in loads:
        c.start()
    for c in taken:
        c.start()
    for i, (_, b, c, _) in enumerate(pieces):
        loads[i].wait()
        c[...] = b[...].astype(F32)
        stores[i].start()
    for a, b in zip(taken, passed):
        a.wait()
        b.start()
    for row, out in (
        (ROW_QB, g_qb), (ROW_VB, g_vb), (ROW_B1, g_b1), (ROW_BP, g_bp), (ROW_G1, g_g1), (ROW_S1, g_s1),
        (ROW_B2, g_b2), (ROW_G2, g_g2), (ROW_S2, g_s2),
    ):
        out[...] = small[row, :]
    for c in range(4):
        g_be[512 * c : 512 * c + 512] = small[ROW_BE + c, :]
    g_w1[...] = small[ROW_W1 : ROW_W1 + 2, :]
    g_w2[...] = small[ROW_W2 : ROW_W2 + 16, :].T
    h0 = lax.broadcasted_iota(jnp.int32, (512, 16), 0) // 32
    h1 = lax.broadcasted_iota(jnp.int32, (512, 16), 1)
    heads = jnp.where(h0 == h1, 1.0, 0.0).astype(BF)
    per_head = sum(nn(jnp.broadcast_to(p, (8, 512)), heads) for p in split3(small[ROW_LS : ROW_LS + 1, :]))
    g_ls[...] = per_head[0, :]
    for c in passed + stores:
        c.wait()


def body(n_img, n_win, inputs, wqkv, qb, vb, hls, w1, b1, w2, wproj, bproj, g1, s1, we, be, wc, bc, g2, s2, cot):
    extra = n_img // 8
    crow, ccol = table_coords()
    dma = pltpu.SemaphoreType.DMA
    n_ar = 15 + (extra - 1)
    n_sm = 8 + (extra - 1)
    vmem = pl.BlockSpec(memory_space=pltpu.VMEM)
    hbm = pl.BlockSpec(memory_space=pl.ANY)
    smem = pl.BlockSpec(memory_space=pltpu.SMEM)
    scratch = [
        pltpu.VMEM((4, TOK, 512), BF),
        pltpu.VMEM((4, TOK, 512), BF),
        pltpu.VMEM((4, TOK, 512), BF),
        pltpu.VMEM((16, 3, 128, 128), F32),
        pltpu.VMEM((4, 4, 4, TOK, TOK), BF),
        pltpu.VMEM((4, 4, TOK, 128), BF),
        pltpu.VMEM((4, 4, TOK, 128), BF),
        pltpu.VMEM((4, 4, TOK, 128), BF),
        pltpu.VMEM((4, 4, TOK, 128), BF),
        pltpu.VMEM((4, 4, TOK, 128), BF),
        pltpu.VMEM((4, 4, TOK, 128), F32),
        pltpu.VMEM((4, TOK, 512), BF),
        pltpu.VMEM((4, TOK, 512), BF),
        pltpu.VMEM((4, 4, 64, 512), BF),
        pltpu.VMEM((4, 4, 64, 512), F32),
        pltpu.VMEM((4, 1024, 512), BF),
        pltpu.VMEM((4, 1024, 512), BF),
        pltpu.VMEM((1024, 512), BF),
        pltpu.VMEM((1024, 512), BF),
        pltpu.VMEM((4, TOK, 512), BF),
        pltpu.VMEM((16, 1024), F32),
        pltpu.VMEM((16, 24, 1024), F32),
        pltpu.VMEM((10, 8, 512), F32),
        pltpu.VMEM((9, 512, 512), BF),
        pltpu.VMEM((9, 496, 512), BF),
        pltpu.VMEM((15, extra - 1, 16, 512) if extra > 1 else (1, 1, 16, 512), BF),
        pltpu.VMEM((512, 1536), BF),
        pltpu.VMEM((512, 512), BF),
        pltpu.VMEM((512, 2048), BF),
        pltpu.VMEM((2048, 512), BF),
        pltpu.VMEM((4, SMALL_ROWS, 512), F32),
        pltpu.VMEM((16, 512), F32),
        pltpu.VMEM((3, 16, 512), F32),
        pltpu.VMEM((3, 16, 512), F32),
        pltpu.VMEM((max(extra - 1, 1), 16, 512), F32),
        pltpu.VMEM((SMALL_ROWS, 512), F32),
        dma((2, 4)), dma((2, 4)), dma((4,)), dma((4,)),
        dma((4,)), dma((4,)), dma((4,)), dma((4,)),
        dma((15, n_ar)), dma((15, n_ar)), dma((15,)),
        dma((n_sm,)), dma((n_sm,)),
        dma((4,)),
    ]
    block = jax.ShapeDtypeStruct(inputs.shape, BF)
    result, grad_inputs, wide, qkv, small = pl.pallas_call(
        functools.partial(block_kernel, n_img, n_win),
        out_shape=(
            block,
            block,
            jax.ShapeDtypeStruct((9, 512, 512), BF),
            jax.ShapeDtypeStruct((2, 3, 512, 256), BF),
            jax.ShapeDtypeStruct((SMALL_ROWS, 512), F32),
        ),
        in_specs=[hbm] * 6 + [vmem] * 2 + [smem] + [vmem] * 12,
        out_specs=(hbm, hbm, hbm, hbm, vmem),
        scratch_shapes=scratch,
        compiler_params=pltpu.CompilerParams(
            collective_id=0, has_side_effects=True, vmem_limit_bytes=64 * 1024 * 1024
        ),
    )(
        inputs, cot, wqkv, wproj, we, wc, qb, vb, hls, w1, b1, w2.T, bproj, g1, s1, be, bc, g2, s2,
        jnp.asarray(crow), jnp.asarray(ccol),
    )
    any_ = lambda shape: jax.ShapeDtypeStruct(shape, F32)
    outs = pl.pallas_call(
        widen_kernel,
        out_shape=(
            block, block, any_((512, 1536)), any_((512,)), any_((512,)), any_((16,)), any_((2, 512)),
            any_((512,)), any_((512, 16)), any_((512, 512)), any_((512,)), any_((512,)), any_((512,)),
            any_((512, 2048)), any_((2048,)), any_((2048, 512)), any_((512,)), any_((512,)), any_((512,)),
        ),
        in_specs=[hbm] * 4 + [vmem],
        out_specs=tuple(hbm if i in (0, 1, 2, 9, 13, 15) else vmem for i in range(19)),
        scratch_shapes=[
            pltpu.VMEM((2,) + inputs.shape, BF),
            pltpu.VMEM((9, 512, 512), BF),
            pltpu.VMEM((6, 512, 256), BF),
            pltpu.VMEM((9, 512, 512), F32),
            pltpu.VMEM((6, 512, 256), F32),
            dma((15,)), dma((15,)), dma((4,)),
        ],
        compiler_params=pltpu.CompilerParams(vmem_limit_bytes=63 * 1024 * 1024),
    )(result, grad_inputs, wide, qkv, small)
    return outs


def solution(mesh):
    n_img, n_win = mesh.shape["img"], mesh.shape["win"]
    block = P("img", "win", None, None)
    return jax.shard_map(
        functools.partial(body, n_img, n_win),
        mesh=mesh,
        in_specs=(block,) + (P(),) * 17 + (block,),
        out_specs=(block, block) + (P(),) * 17,
        check_vma=False,
    )
```

time: 202 us -> 150 us (0.74)
  Pallas kernels: 169 us -> 148 us
  local copies, waits for them, and re-layouts: 22.2 us -> 1.67 us
  other arithmetic: 9.87 us -> 0 us
    pallas_call x1, Pallas kernels: 169 us -> 138 us  [body(): pl.pallas_call(functools.partial(block_kernel, n_img, n_win), out_shape=(...]
    pallas_call x0 -> x1, Pallas kernels: none -> 9.54 us  [body(): pl.pallas_call(widen_kernel, out_shape=(block, block, any_((512, 1536)),...]
    unnamed x14 -> x0, local copies, waits for them, and re-layouts: 9.31 us -> none
    convert_element_type x1 -> x0, other arithmetic: 9.24 us -> none  [body(): sums = sums.astype(F32)]
    slice x4 -> x0, local copies, waits for them, and re-layouts: 6.65 us -> none  [the longest x1 3.35 us: body(): fc2 = sums[0].reshape(2048, 512)]
    reshape x1 -> x0, local copies, waits for them, and re-layouts: 2.45 us -> none  [body(): jnp.transpose(sums[1].reshape(4, 512, 512), (1, 0, 2)).reshape(512, 2048)]
    squeeze x1 -> x0, local copies, waits for them, and re-layouts: 2.26 us -> none  [body(): proj = sums[2, 1, 512:]]
where the time goes in v1:
time: 150 us
  Pallas kernels  148 us (99%)
  local copies, waits for them, and re-layouts  1.67 us (1%)
    pallas_call x1, Pallas kernels, body(): pl.pallas_call(functools.partial(block_kernel, n_img, n_win), out_shape=(...  138 us
    pallas_call x1, Pallas kernels, body(): pl.pallas_call(widen_kernel, out_shape=(block, block, any_((512, 1536)),...  9.54 us

profile of v1, /device:TPU:0, one launch (start us, length us, event | category | flops | bytes accessed | tf_op | source)
XLA Modules:
  0.0 149.9 jit_solution(12830396937266847254)
XLA Ops:
  0.7 138.0 %shard_map.348 = (bf16[4,1,256,512]{3,2,1,0:T(8,128)(2,1)}, bf16[4,1,256,512]{3,2,1,0:T(8,128)(2,1)}, bf16[9,512,512]{2,1,0:T(8,128)(2,1)}, bf16[2,3,512,256]{3,2,1,0:T(8,128)(2,1)}, f32[32,512]{1,0:T(8,128)}) custom-call(bf16[4,1,256,512]{3,2,1,0:T(8,128)(2,1)} %x_hbm.1, bf16[4,1,256,512]{3,2,1,0:T(8,128)(2,1)} %cot_hbm.1, bf16[512,1536]{1,0:T(8,128)(2,1)} %wqkv_hbm.1, ...), custom_call_target="tpu_custom_call" | custom-call | tf_op jit(solution)/shard_map/pallas_call | solution.py:946
  138.7 9.5 %shard_map.349 = (bf16[4,1,256,512]{3,2,1,0:T(8,128)(2,1)}, bf16[4,1,256,512]{3,2,1,0:T(8,128)(2,1)}, f32[512,1536]{1,0:T(8,128)}, f32[512]{0:T(512)}, f32[512]{...) custom-call(bf16[4,1,256,512]{3,2,1,0:T(8,128)(2,1)} %get-tuple-elem, ...), custom_call_target="tpu_custom_call" | custom-call | tf_op jit(solution)/shard_map/pallas_call | solution.py:966
  148.2 1.7 %copy.40 = f32[512,16]{0,1:T(8,128)} copy(f32[512,16]{1,0:T(8,128)} %get-tuple-element.37) | data formatting | bytes 65536 | tf_op jit(solution)/shard_map/pallas_call | solution.py:966

commit v2 on v1

--- a/solution.py
+++ b/solution.py
@@ -26,29 +26,34 @@
 
 SCHEDULE = {
     "a1": ((0, 0),),
-    "a3": ((1, 0), (0, 1)),
-    "d0": ((1, 1),),
-    "d1": ((0, 2),),
-    "d2": ((1, 2),),
-    "d3": ((0, 3),),
-    "b0": ((1, 3),),
-    "b1": ((2, 0),),
-    "b3": ((3, 0), (2, 1)),
-    "gproj": ((4, 0), (3, 1), (0, 4), (4, 1)),
-    "r0": ((1, 4), (2, 2), (3, 2), (0, 5)),
-    "r1": ((4, 2), (2, 3), (1, 5), (3, 3)),
-    "r2": ((0, 6), (4, 3), (1, 6), (2, 4)),
-    "r3": ((3, 4), (0, 7)),
-    "gq0": ((5, 0), (4, 4), (0, 8), (1, 7), (5, 1)),
-    "r4": ((1, 8), (2, 5)),
-    "r5": ((3, 5), (4, 5), (5, 2), (2, 6)),
-    "r6": ((3, 6), (4, 6), (5, 3)),
-    "r7": ((2, 7),),
-    "gq1": ((6, 0), (5, 4), (3, 7), (2, 8), (6, 1), (4, 7), (3, 8), (4, 8)),
-    "bb": ((5, 5),),
-    "net": ((7, 0), (5, 6), (6, 2), (7, 1)),
-    "end": ((6, 3), (6, 4), (7, 2), (6, 5), (7, 3), (6, 6), (7, 4)),
+    "a3": ((1, 0),),
+    "d0": ((0, 1), (1, 1)),
+    "d1": ((2, 0),),
+    "d2": ((2, 1),),
+    "d3": ((3, 0),),
+    "nb": ((1, 2), (0, 2)),
+    "gproj": ((4, 0), (3, 1)),
+    "r0": ((4, 1), (0, 3), (1, 3)),
+    "r1": ((2, 2), (3, 2)),
+    "r2": ((4, 2), (0, 4)),
+    "r3": ((2, 3), (1, 4)),
+    "gq0": ((5, 0), (4, 3), (3, 3)),
+    "r4": ((5, 1), (0, 5), (2, 4)),
+    "r6": ((1, 5), (4, 4)),
+    "r7": ((3, 4), (5, 2), (2, 5), (0, 6)),
+    "gq1": ((6, 0), (4, 5), (1, 6)),
+    "puts": ((6, 1), (2, 6), (3, 5)),
+    "bb": ((5, 3), (4, 6)),
+    "net": ((7, 0),),
+    "end": (
+        (7, 1), (1, 7), (0, 7), (1, 8), (0, 8), (6, 2), (3, 6), (5, 4), (2, 7), (4, 7), (6, 3), (2, 8), (7, 2),
+        (4, 8), (3, 7), (6, 4), (3, 8), (5, 5), (7, 3), (5, 6), (7, 4), (6, 5), (6, 6),
+    ),
 }
+ORDERS = (
+    "zxy", "yxz", "xyz", "xyz", "zxy", "xyz", "yzx", "xyz", "yxz",
+    "pz", "pz", "pz", "pz", "pz", "pz",
+)
 
 
 def nn(a, b):
@@ -170,6 +175,11 @@
         for i, (a, b) in enumerate(((wqkv_hbm, wqkv), (wproj_hbm, wproj), (we_hbm, we), (wc_hbm, wc)))
     ]
 
+    own_x = pltpu.make_async_copy(x_hbm.at[me, 0], xr.at[me], r_x.at[0, 0])
+    own_c = pltpu.make_async_copy(cot_hbm.at[me, 0], cr.at[me], r_c.at[0])
+    for c in [own_x] + weights + [own_c]:
+        c.start()
+
     barrier = pltpu.get_barrier_semaphore()
     others = [ring_to(k) for k in range(1, n_win)] + [x_peer, (img + 1 - 2 * xpos, lax.rem(me + 2, 4))]
     others += [z_peer(k) for k in range(1, 4)] + [far_peer(k) for k in range(1, extra)]
@@ -190,9 +200,6 @@
         frm = ring_from(k)
         return remote(src_hbm.at[frm, 0], dst.at[frm], ssem.at[k], rsem.at[k], ring_to(k))
 
-    def own_part(src_hbm, dst, sem):
-        return pltpu.make_async_copy(src_hbm.at[me, 0], dst.at[me], sem.at[0])
-
     def half_rows(w, half):
         return pl.ds(pl.multiple_of(128 * (1 - w // 2 if half == 0 else w // 2), 128), 128)
 
@@ -210,10 +217,8 @@
     for half in range(2):
         for k in (2, 1, 3):
             x_send(k, half).start()
-    own_x = own_part(x_hbm, xr, r_x.at[0])
-    own_x.start()
-    for c in weights:
-        c.start()
+    for k in (2, 1, 3):
+        spread(cot_hbm, cr, s_c, r_c, k).start()
 
     def net_piece(c):
         rows = pl.ds(pl.multiple_of(256 * c, 256), 256)
@@ -270,11 +275,40 @@
 
         lax.fori_loop(0, 4, one, 0)
 
+    def project(half):
+        xw = xroll[2 * half : 2 * half + 2].reshape(512, 512)
+
+        def one(p, _):
+            def cols(i):
+                return pl.ds(pl.multiple_of(512 * i + 256 * p, 256), 256)
+
+            q = nn(xw, wqkv[:, cols(0)]) + qb[cols(0)][None, :]
+            qi = lax.rsqrt(nn((q * q).astype(BF), head_ones) + EPS_DIR)
+            qsc = (q * qi * scale_lanes(p)).astype(BF)
+            k = nn(xw, wqkv[:, cols(1)])
+            ki = lax.rsqrt(nn((k * k).astype(BF), head_ones) + EPS_DIR)
+            kn = (k * ki).astype(BF)
+            v = (nn(xw, wqkv[:, cols(2)]) + vb[cols(0)][None, :]).astype(BF)
+            for w in range(2):
+                rows = slice(256 * w, 256 * w + 256)
+                for i in range(2):
+                    lanes = slice(128 * i, 128 * i + 128)
+                    at = (2 * half + w, 2 * p + i)
+                    qs[at] = qsc[rows, lanes]
+                    kl[at] = kn[rows, lanes]
+                    vl[at] = v[rows, lanes]
+                    qinv[at] = qi[rows, lanes].astype(BF)
+                    kinv[at] = ki[rows, lanes].astype(BF)
+            return 0
+
+        lax.fori_loop(0, 2, one, 0)
+
     own_x.wait()
     for k in (1, 2, 3):
         x_arrival(k, 0).wait_recv()
     lay(0)
     weights[0].wait()
+    project(0)
     weights[1].wait()
 
     row_half = lax.broadcasted_iota(jnp.int32, (128, 128), 0) // 64
@@ -282,35 +316,17 @@
     apart = jnp.where(row_half == col_half, 0.0, MASK_FILL)
 
     def home(o, bcol, br):
-        return lax.rem(2 * (o // 2) + br + 1, 4), lax.rem(2 * lax.rem(o, 2) + bcol + 1, 4)
+        row, col = lax.rem(2 * (o // 2) + br + 1, 4), lax.rem(2 * lax.rem(o, 2) + bcol + 1, 4)
+        return 2 * (row // 2) + col // 2, 2 * lax.rem(row, 2) + lax.rem(col, 2)
 
     def attend(o, _):
         @pl.when(o == 2)
         def _():
             for k in (1, 2, 3):
                 x_arrival(k, 1).wait_recv()
-            for k in (2, 1, 3):
-                spread(cot_hbm, cr, s_c, r_c, k).start()
-            own_part(cot_hbm, cr, r_c).start()
             lay(1)
-
-        xw = xroll[o]
-        for p in range(2):
-            cols = slice(256 * p, 256 * p + 256)
-            q = nn(xw, wqkv[:, cols]) + qb[cols][None, :]
-            qi = lax.rsqrt(nn((q * q).astype(BF), head_ones) + EPS_DIR)
-            qsc = (q * qi * scale_lanes(p)).astype(BF)
-            k = nn(xw, wqkv[:, 512 + 256 * p : 768 + 256 * p])
-            ki = lax.rsqrt(nn((k * k).astype(BF), head_ones) + EPS_DIR)
-            kn = (k * ki).astype(BF)
-            v = (nn(xw, wqkv[:, 1024 + 256 * p : 1280 + 256 * p]) + vb[cols][None, :]).astype(BF)
-            for i in range(2):
-                half = slice(128 * i, 128 * i + 128)
-                qs[o, 2 * p + i] = qsc[:, half]
-                kl[o, 2 * p + i] = kn[:, half]
-                vl[o, 2 * p + i] = v[:, half]
-                qinv[o, 2 * p + i] = qi[:, half].astype(BF)
-                kinv[o, 2 * p + i] = ki[:, half].astype(BF)
+            project(1)
+
         rows_cut = jnp.where(o // 2 == 1, apart, 0.0)
         cols_cut = jnp.where(lax.rem(o, 2) == 1, jnp.full((128, 128), MASK_FILL, F32), rows_cut)
 
@@ -343,17 +359,11 @@
         for bcol in range(2):
             for br in range(2):
                 at = (bcol * 2 + br) * 64
-                brow, bc_ = home(o, bcol, br)
-                blk[brow, bc_] = branch[at : at + 64, :]
+                blk[home(o, bcol, br)] = branch[at : at + 64, :]
         return 0
 
     lax.fori_loop(0, 4, attend, 0)
 
-    for k in (0, 1, 2, 3):
-        if k == 0:
-            own_part(cot_hbm, cr, r_c).wait()
-        else:
-            spread_in(cot_hbm, cr, s_c, r_c, k).wait_recv()
     weights[2].wait()
     weights[3].wait()
     acc_s[...] = jnp.zeros_like(acc_s)
@@ -364,43 +374,57 @@
     def flat(quads):
         return jnp.concatenate([quads[0][0], quads[0][1], quads[1][0], quads[1][1]], axis=0)
 
-    def first_norm(w):
-        wr, wcol = w // 2, lax.rem(w, 2)
-        back = jnp.concatenate(
-            [blk[2 * wr + qr, 2 * wcol + qc] for qr in range(2) for qc in range(2)], axis=0
-        ).astype(F32)
+    def first_norm(pair):
+        back = blk[pl.ds(2 * pair, 2)].reshape(512, 512).astype(F32)
         ctr = back - jnp.mean(back, axis=1, keepdims=True)
         r1 = lax.rsqrt(jnp.mean(ctr * ctr, axis=1, keepdims=True) + EPS_NORM)
         return ctr * r1, r1
 
-    def dense(w, _):
-        e = flat(to_blocks(cr[w].astype(F32)))
-        z1, _ = first_norm(w)
-        middle = flat(to_blocks(xr[w].astype(F32))) + z1 * g1[...][None, :] + s1[...][None, :]
+    def laid(ref, pair):
+        return jnp.concatenate([flat(to_blocks(ref[2 * pair + i].astype(F32))) for i in range(2)], axis=0)
+
+    def dense(turn, _):
+        pair = lax.rem(ypos + turn, 2)
+        z1, _ = first_norm(pair)
+        middle = laid(xr, pair) + z1 * g1[...][None, :] + s1[...][None, :]
         ml = middle.astype(BF)
-        rows = pl.ds(pl.multiple_of(w * TOK, TOK), TOK)
+        rows = pl.ds(pl.multiple_of(pair * 512, 512), 512)
         mlow[rows, :] = ml
-        out = jnp.zeros((TOK, 512), F32)
-        for c in range(4):
-            cols = slice(512 * c, 512 * c + 512)
+        out = jnp.zeros((512, 512), F32)
+        for c in range(8):
+            cols = slice(256 * c, 256 * c + 256)
+            part_cols = slice(256 * (c % 2), 256 * (c % 2) + 256)
             hid = nn(ml, we[:, cols]) + be[cols][None, :]
             cap, low = gelu_parts(hid)
             a = (hid * cap).astype(BF)
-            act[c, rows, :] = a
-            dhid[c, rows, :] = (cap + hid * low).astype(BF)
+            act[c // 2, rows, part_cols] = a
+            dhid[c // 2, rows, part_cols] = (cap + hid * low).astype(BF)
             out = out + nn(a, wc[cols, :])
         out = out + bc[...][None, :]
         ctr2 = out - jnp.mean(out, axis=1, keepdims=True)
         r2 = lax.rsqrt(jnp.mean(ctr2 * ctr2, axis=1, keepdims=True) + EPS_NORM)
         z2 = ctr2 * r2
         result = middle + z2 * g2[...][None, :] + s2[...][None, :]
-        quads = [[result[128 * qr + 64 * qc : 128 * qr + 64 * qc + 64] for qc in range(2)] for qr in range(2)]
-        xr[w] = from_blocks(quads).astype(BF)
-
-        @pl.when(w != me)
+        for i in range(2):
+            quads = [[result[256 * i + 64 * (2 * qr + qc) :][:64] for qc in range(2)] for qr in range(2)]
+            w = 2 * pair + i
+            xr[w] = from_blocks(quads).astype(BF)
+
+            @pl.when(w != me)
+            def _(w=w):
+                res_copy(w).start()
+
+        @pl.when(turn == 0)
         def _():
-            res_copy(w).start()
-
+            own_c.wait()
+            spread_in(cot_hbm, cr, s_c, r_c, 3 - 2 * core).wait_recv()
+
+        @pl.when(turn == 1)
+        def _():
+            spread_in(cot_hbm, cr, s_c, r_c, 2).wait_recv()
+            spread_in(cot_hbm, cr, s_c, r_c, 1 + 2 * core).wait_recv()
+
+        e = laid(cr, pair)
         acc_s[0] += col_sum(e * z2)
         acc_s[1] += col_sum(e)
         dn = e * g2[...][None, :]
@@ -412,7 +436,7 @@
         acc_s[2] += col_sum(do.astype(F32))
         return 0
 
-    lax.fori_loop(0, 4, dense, 0)
+    lax.fori_loop(0, 2, dense, 0)
     own_res = pltpu.make_async_copy(xr.at[me], res_hbm.at[me, 0], r_res.at[me])
     own_res.start()
 
@@ -540,8 +564,7 @@
     def together(units):
         return [lambda steps=steps: [step() for step in steps] for steps in zip(*units)]
 
-    orders = ("xyz", "yxz")
-    wide_units = [sum_unit(a, asum.at[a], rec.at[a], wide_hbm.at[a], orders[a % 2]) for a in range(9)]
+    wide_units = [sum_unit(a, asum.at[a], rec.at[a], wide_hbm.at[a], ORDERS[a]) for a in range(9)]
     groups = [together(wide_units[2 * i : 2 * i + 2]) for i in range(4)] + [wide_units[8]]
     for p in range(2):
         part_units = []
@@ -550,7 +573,7 @@
             part_units.append(
                 sum_unit(
                     9 + 3 * p + i, act.at[p].at[place], act.at[2 + p].at[place], qkv_hbm.at[p, i],
-                    "pz",
+                    ORDERS[9 + 3 * p + i],
                 )
             )
         groups.append(together(part_units))
@@ -640,37 +663,35 @@
         asum[c] = tn(act[c], dout[...]).astype(BF)
         run(f"a{c}")
 
-    def dense_back(w, _):
-        wr, wcol = w // 2, lax.rem(w, 2)
-        rows = pl.ds(pl.multiple_of(w * TOK, TOK), TOK)
-        do = dout[rows, :]
-        dm = flat(to_blocks(cr[w].astype(F32)))
-        for c in range(4):
-            cols = slice(512 * c, 512 * c + 512)
-            dh = (nt(do, wc[cols, :]) * dhid[c, rows, :].astype(F32)).astype(BF)
-            dhid[c, rows, :] = dh
-            acc_s[3 + c] += col_sum(dh.astype(F32))
-            dm = dm + nt(dh, we[:, cols])
-        z1, r1 = first_norm(w)
+    for w in range(4):
+        dmid[w] = flat(to_blocks(cr[w].astype(F32))).reshape(4, 64, 512)
+
+    def dense_back(c, _):
+        cols = pl.ds(pl.multiple_of(512 * c, 512), 512)
+        dh = (nt(dout[...], wc[cols, :]) * dhid[c].astype(F32)).astype(BF)
+        dhid[c] = dh
+        acc_s[3 + c] = col_sum(dh.astype(F32))
+        dmid[...] += nt(dh, we[:, cols]).reshape(4, 4, 64, 512)
+        asum[4 + c] = tn(mlow[...], dh).astype(BF)
+        run_in("d", c)
+        return 0
+
+    lax.fori_loop(0, 4, dense_back, 0)
+
+    def norm_back(pair, _):
+        z1, r1 = first_norm(pair)
+        dm = dmid[pl.ds(2 * pair, 2)].reshape(512, 512)
         acc_s[7] += col_sum(dm * z1)
         acc_s[8] += col_sum(dm)
         dn1 = dm * g1[...][None, :]
         db = r1 * (
             dn1 - jnp.mean(dn1, axis=1, keepdims=True) - z1 * jnp.mean(dn1 * z1, axis=1, keepdims=True)
         )
-        db = db.astype(BF)
-        for qr in range(2):
-            for qc in range(2):
-                at = 128 * qr + 64 * qc
-                dmid[2 * wr + qr, 2 * wcol + qc] = dm[at : at + 64]
-                blk[2 * wr + qr, 2 * wcol + qc] = db[at : at + 64]
-        run_in("d", w)
+        blk[pl.ds(2 * pair, 2)] = db.astype(BF).reshape(2, 4, 64, 512)
         return 0
 
-    lax.fori_loop(0, 4, dense_back, 0)
-    for c in range(4):
-        asum[4 + c] = tn(mlow[...], dhid[c]).astype(BF)
-        run(f"b{c}")
+    lax.fori_loop(0, 2, norm_back, 0)
+    run("nb")
 
     bias[...] = jnp.zeros_like(bias)
 
@@ -678,8 +699,7 @@
         for bcol in range(2):
             for br in range(2):
                 at = (bcol * 2 + br) * 64
-                brow, bc_ = home(o, bcol, br)
-                cr[o, at : at + 64, :] = blk[brow, bc_]
+                cr[o, at : at + 64, :] = blk[home(o, bcol, br)]
         return 0
 
     lax.fori_loop(0, 4, gather, 0)
@@ -732,19 +752,19 @@
             dhid[0, rows, lanes] = (qinv[o, g].astype(F32) * (scale * dq - (1.0 / scale) * qf * aq)).astype(BF)
             dhid[1, rows, lanes] = (kinv[o, g].astype(F32) * (dk - kf * ak)).astype(BF)
             dhid[2, rows, lanes] = dv.astype(BF)
-        moved = sum(
-            nt(dhid[i, rows, half], wqkv[:, pl.ds(pl.multiple_of(512 * i + 256 * p, 256), 256)])
-            for i in range(3)
-        )
-        for bcol in range(2):
-            for br in range(2):
-                at = (bcol * 2 + br) * 64
-                brow, bc_ = home(o, bcol, br)
-                dmid[brow, bc_] += moved[at : at + 64, :]
         run_in("r", it)
 
         @pl.when(lax.rem(it, 4) == 3)
         def _():
+            moved = sum(
+                nt(dhid[i, :, half], wqkv[:, pl.ds(pl.multiple_of(512 * i + 256 * p, 256), 256)])
+                for i in range(3)
+            )
+            for w in range(4):
+                for bcol in range(2):
+                    for br in range(2):
+                        at = 256 * w + (bcol * 2 + br) * 64
+                        dmid[home(w, bcol, br)] += moved[at : at + 64, :]
             xflat = xroll[...].reshape(1024, 512)
             for i in range(3):
                 grad = tn(xflat, dhid[i, :, half]).astype(BF)
@@ -759,8 +779,7 @@
         return remote(slope.at[w], gin_hbm.at[me, 0], s_gin.at[w], r_gin.at[me], (img, w))
 
     def finish(w, _):
-        wr, wcol = w // 2, lax.rem(w, 2)
-        quads = [[dmid[2 * wr + qr, 2 * wcol + qc] for qc in range(2)] for qr in range(2)]
+        quads = [[dmid[w, 2 * qr + qc] for qc in range(2)] for qr in range(2)]
         slope[w] = from_blocks(quads).astype(BF)
 
         @pl.when(w != me)

time: 150 us -> 133 us (0.89)
  Pallas kernels: 148 us -> 131 us
    pallas_call x1, Pallas kernels: 138 us -> 121 us  [body(): pl.pallas_call(functools.partial(block_kernel, n_img, n_win), out_shape=(...]
where the time goes in v2:
time: 133 us
  Pallas kernels  131 us (98%)
  local copies, waits for them, and re-layouts  1.67 us (1%)
    pallas_call x1, Pallas kernels, body(): pl.pallas_call(functools.partial(block_kernel, n_img, n_win), out_shape=(...  121 us
    pallas_call x1, Pallas kernels, body(): pl.pallas_call(widen_kernel, out_shape=(block, block, any_((512, 1536)),...  9.54 us

profile of v2, /device:TPU:0, one launch (start us, length us, event | category | flops | bytes accessed | tf_op | source)
XLA Modules:
  0.0 133.0 jit_solution(9962272574190215692)
XLA Ops:
  0.7 121.1 %shard_map.348 = (bf16[4,1,256,512]{3,2,1,0:T(8,128)(2,1)}, bf16[4,1,256,512]{3,2,1,0:T(8,128)(2,1)}, bf16[9,512,512]{2,1,0:T(8,128)(2,1)}, bf16[2,3,512,256]{3,2,1,0:T(8,128)(2,1)}, f32[32,512]{1,0:T(8,128)}) custom-call(bf16[4,1,256,512]{3,2,1,0:T(8,128)(2,1)} %x_hbm.1, bf16[4,1,256,512]{3,2,1,0:T(8,128)(2,1)} %cot_hbm.1, bf16[512,1536]{1,0:T(8,128)(2,1)} %wqkv_hbm.1, ...), custom_call_target="tpu_custom_call" | custom-call | tf_op jit(solution)/shard_map/pallas_call | solution.py:965
  121.8 9.5 %shard_map.349 = (bf16[4,1,256,512]{3,2,1,0:T(8,128)(2,1)}, bf16[4,1,256,512]{3,2,1,0:T(8,128)(2,1)}, f32[512,1536]{1,0:T(8,128)}, f32[512]{0:T(512)}, f32[512]{...) custom-call(bf16[4,1,256,512]{3,2,1,0:T(8,128)(2,1)} %get-tuple-elem, ...), custom_call_target="tpu_custom_call" | custom-call | tf_op jit(solution)/shard_map/pallas_call | solution.py:985
  131.3 1.7 %copy.40 = f32[512,16]{0,1:T(8,128)} copy(f32[512,16]{1,0:T(8,128)} %get-tuple-element.37) | data formatting | bytes 65536 | tf_op jit(solution)/shard_map/pallas_call | solution.py:985

commit v3 on v2

--- a/solution.py
+++ b/solution.py
@@ -26,33 +26,31 @@
 
 SCHEDULE = {
     "a1": ((0, 0),),
-    "a3": ((1, 0),),
-    "d0": ((0, 1), (1, 1)),
-    "d1": ((2, 0),),
-    "d2": ((2, 1),),
-    "d3": ((3, 0),),
-    "nb": ((1, 2), (0, 2)),
-    "gproj": ((4, 0), (3, 1)),
-    "r0": ((4, 1), (0, 3), (1, 3)),
-    "r1": ((2, 2), (3, 2)),
-    "r2": ((4, 2), (0, 4)),
-    "r3": ((2, 3), (1, 4)),
-    "gq0": ((5, 0), (4, 3), (3, 3)),
-    "r4": ((5, 1), (0, 5), (2, 4)),
-    "r6": ((1, 5), (4, 4)),
-    "r7": ((3, 4), (5, 2), (2, 5), (0, 6)),
-    "gq1": ((6, 0), (4, 5), (1, 6)),
-    "puts": ((6, 1), (2, 6), (3, 5)),
-    "bb": ((5, 3), (4, 6)),
-    "net": ((7, 0),),
-    "end": (
-        (7, 1), (1, 7), (0, 7), (1, 8), (0, 8), (6, 2), (3, 6), (5, 4), (2, 7), (4, 7), (6, 3), (2, 8), (7, 2),
-        (4, 8), (3, 7), (6, 4), (3, 8), (5, 5), (7, 3), (5, 6), (7, 4), (6, 5), (6, 6),
-    ),
+    "a3": ((1, 0), (0, 1)),
+    "d0": ((1, 1),),
+    "d1": ((2, 0), (0, 2)),
+    "d2": ((2, 1), (1, 2)),
+    "d3": ((3, 0), (0, 3)),
+    "nb": ((3, 1), (2, 2)),
+    "gproj": ((4, 0), (1, 3), (0, 4)),
+    "r0": ((4, 1), (0, 5), (2, 3), (1, 4)),
+    "r1": ((3, 2),),
+    "r2": ((1, 5), (4, 2), (2, 4), (0, 6)),
+    "r3": ((3, 3),),
+    "gq0": ((5, 0), (1, 6), (4, 3), (2, 5), (5, 1), (3, 4)),
+    "r4": ((0, 7), (1, 7)),
+    "r5": ((4, 4), (5, 2), (2, 6), (3, 5), (1, 8)),
+    "r6": ((0, 8),),
+    "r7": ((4, 5), (5, 3), (2, 7)),
+    "gq1": ((6, 0), (3, 6), (4, 6), (1, 9), (6, 1), (5, 4), (1, 10), (0, 9), (3, 7)),
+    "finish": ((2, 8), (0, 10)),
+    "bb": ((6, 2), (5, 5), (3, 8)),
+    "net": ((7, 0), (2, 9), (7, 1)),
+    "end": ((6, 3), (2, 10), (3, 9), (5, 6), (3, 10), (6, 4), (7, 2), (5, 7), (5, 8), (7, 3), (6, 5), (7, 4), (6, 6)),
 }
 ORDERS = (
-    "zxy", "yxz", "xyz", "xyz", "zxy", "xyz", "yzx", "xyz", "yxz",
-    "pz", "pz", "pz", "pz", "pz", "pz",
+    "wvxy", "xwvy", "xywv", "yxwv", "xywv", "wvxy", "xwyv", "xwyv", "pz",
+    "xzy", "yxz", "xzy", "pz", "pz", "pz",
 )
 
 
@@ -121,9 +119,7 @@
     rows = np.zeros((8, 1024), np.float32)
     rows[0:2] = out
     rows[2] = 1.0
-    cols = np.zeros((1024, 8), np.float32)
-    cols[:, 0:2] = out.T
-    return rows, cols
+    return rows
 
 
 def net_first(cols, w1, b1):
@@ -132,13 +128,14 @@
 
 def block_kernel(
     n_img, n_win,
-    x_hbm, cot_hbm, wqkv_hbm, wproj_hbm, we_hbm, wc_hbm, qb, vb, hls, w1, b1, w2t, bproj, g1, s1, be, bc, g2, s2,
-    crow, ccol,
+    x_hbm, cot_hbm, wqkv_hbm, wproj_hbm, we_hbm, wc_hbm, hls, qb_hbm, vb_hbm, w1_hbm, b1_hbm,
+    w2t_hbm, bproj_hbm, g1_hbm, s1_hbm, be_hbm, bc_hbm, g2_hbm, s2_hbm, crow_hbm,
     res_hbm, gin_hbm, wide_hbm, qkv_hbm, small_out,
     xr, cr, xroll, bias, ex, qs, kl, vl, qinv, kinv, isum, mixed, mixlo, blk, dmid, act, dhid, dout,
     mlow, slope, tab, part, acc_s, asum, rec, far, wqkv, wproj, we, wc,
+    qb, vb, w1, b1, w2t, bproj, g1, s1, be, bc, g2, s2, crow,
     small_s, small_c, small_p, small_z, small_far, small_o,
-    s_x, r_x, s_c, r_c, s_res, r_res, s_gin, r_gin, s_ar, r_ar, l_ar, s_sm, r_sm, s_w,
+    s_x, r_x, s_c, r_c, s_res, r_res, s_gin, r_gin, s_ar, r_ar, l_ar, s_sm, r_sm, s_w, s_v,
 ):
     img = lax.axis_index("img")
     me = lax.axis_index("win")
@@ -177,7 +174,17 @@
 
     own_x = pltpu.make_async_copy(x_hbm.at[me, 0], xr.at[me], r_x.at[0, 0])
     own_c = pltpu.make_async_copy(cot_hbm.at[me, 0], cr.at[me], r_c.at[0])
-    for c in [own_x] + weights + [own_c]:
+    vectors = [
+        pltpu.make_async_copy(a, b, s_v.at[i])
+        for i, (a, b) in enumerate(
+            (
+                (w1_hbm, w1), (b1_hbm, b1), (w2t_hbm, w2t), (crow_hbm, crow), (qb_hbm, qb), (vb_hbm, vb),
+                (bproj_hbm, bproj), (g1_hbm, g1), (s1_hbm, s1), (be_hbm, be), (bc_hbm, bc), (g2_hbm, g2),
+                (s2_hbm, s2),
+            )
+        )
+    ]
+    for c in vectors + [own_x] + weights + [own_c]:
         c.start()
 
     barrier = pltpu.get_barrier_semaphore()
@@ -220,9 +227,11 @@
     for k in (2, 1, 3):
         spread(cot_hbm, cr, s_c, r_c, k).start()
 
+    for c in vectors:
+        c.wait()
     def net_piece(c):
         rows = pl.ds(pl.multiple_of(256 * c, 256), 256)
-        return rows, net_first(ccol[rows, :], w1[...], b1[...][None, :])
+        return rows, net_first(crow[:, rows].T, w1[...], b1[...][None, :])
 
     def look_up(c, _):
         cols, pre = net_piece(c)
@@ -440,23 +449,29 @@
     own_res = pltpu.make_async_copy(xr.at[me], res_hbm.at[me, 0], r_res.at[me])
     own_res.start()
 
-    digits = {"x": (xpos, 2), "y": (ypos, 2), "z": (zpos, 4), "p": (plane_pos, 4)}
+    digits = {
+        "x": (xpos, 2), "y": (ypos, 2), "z": (zpos, 4), "p": (plane_pos, 4),
+        "w": (lax.rem(zpos, 2), 2), "v": (zpos // 2, 2),
+    }
 
     def digit_peer(d, k):
         if d == "z":
             return z_peer(k)
         if d == "p":
             return plane_peer(k)
+        z_step = {"w": 1 - 2 * lax.rem(zpos, 2), "v": 2 - 4 * (zpos // 2)}
+        if d in z_step:
+            return (img + 2 * z_step[d], me)
         return x_peer if d == "x" else y_peer
 
     def sum_unit(a, src, land, out, order):
         n = src.shape[1]
-        levels, at, size, room, sem = [], core * 256, 256, 256, 1
+        levels, at, size, room = [], core * 256, 256, 256
         for d in order:
             pos, count = digits[d]
             part_size = size // count
-            levels.append((d, pos, count, at, part_size, room, sem))
-            at, room, sem = at + pos * part_size, room + (count - 1) * part_size, sem + count - 1
+            levels.append((d, pos, count, at, part_size, room))
+            at, room = at + pos * part_size, room + (count - 1) * part_size
             size = part_size
         own_at, last = at, len(order) - 1
 
@@ -464,34 +479,48 @@
             return pl.ds(pl.multiple_of(start, 16), length)
 
         def copy(src_at, dst, length, i, peer):
-            return remote(src.at[rows(src_at, length)], dst, s_ar.at[a, i], r_ar.at[a, i], peer)
+            return remote(src.at[rows(src_at, length)], dst, s_ar.at[a, 0], r_ar.at[a, i], peer)
 
         def core_send():
             return copy((1 - core) * 256, land.at[pl.ds(0, 256)], 256, 0, core_peer)
 
         def down(j, k):
-            d, pos, count, at, length, room, sem = levels[j]
+            d, pos, count, at, length, room = levels[j]
             dst = land.at[pl.ds(room + (k - 1) * length, length)]
-            return copy(at + lax.rem(pos + k, count) * length, dst, length, sem + k - 1, digit_peer(d, k))
-
-        def up(j, k, pos):
-            d, _, count, at, length, _, sem = levels[j]
+            return copy(at + lax.rem(pos + k, count) * length, dst, length, 1 + j, digit_peer(d, k))
+
+        def all_down(j):
+            d, _, count, _, length, room = levels[j]
+            dst = land.at[pl.ds(room, (count - 1) * length)]
+            return copy(0, dst, (count - 1) * length, 1 + j, digit_peer(d, 1))
+
+        def up(j, k):
+            d, pos, count, at, length, _ = levels[j]
             here = out.at[rows(at + pos * length, length)]
             from_ = src.at[rows(own_at, length)] if j == last else here
-            return remote(from_, here, s_ar.at[a, 6 + sem + k], r_ar.at[a, 6 + sem + k], digit_peer(d, k))
+            return remote(from_, here, s_ar.at[a, 1], r_ar.at[a, 5 + j], digit_peer(d, k))
+
+        def all_up(j):
+            d, _, count, _, length, _ = levels[j]
+            some = out.at[pl.ds(0, (count - 1) * length)]
+            return remote(some, some, s_ar.at[a, 1], r_ar.at[a, 5 + j], digit_peer(d, 1))
 
         def core_up(c):
             here = out.at[rows(c * 256, 256)]
-            return remote(here, here, s_ar.at[a, 14], r_ar.at[a, 14], core_peer)
+            return remote(here, here, s_ar.at[a, 1], r_ar.at[a, 9], core_peer)
+
+        def all_sent(i):
+            some = out.at[pl.ds(0, 496)]
+            return remote(some, some, s_ar.at[a, i], r_ar.at[a, 0], core_peer)
 
         def far_send(k):
-            return copy(own_at, far.at[a, k - 1, :, 0:n], 16, 15 + k - 1, far_peer(k))
+            return remote(
+                src.at[rows(own_at, 16)], far.at[a, k - 1, :, 0:n], s_ar.at[a, 1 + k], r_ar.at[a, 9 + k],
+                far_peer(k),
+            )
 
         def peers(j):
             return range(1, levels[j][2])
-
-        def from_pos(j, k):
-            return lax.rem(levels[j][1] + levels[j][2] - k, levels[j][2])
 
         def local():
             here = rows(own_at, 16)
@@ -511,10 +540,9 @@
                 down(j, k).start()
 
         def take(j):
-            d, pos, count, at, length, room, sem = levels[j]
+            d, pos, count, at, length, room = levels[j]
             here = rows(at + pos * length, length)
-            for k in peers(j):
-                down(j, k).wait_recv()
+            all_down(j).wait_recv()
             total = src[here, :].astype(F32)
             for k in peers(j):
                 r = room + (k - 1) * length
@@ -533,30 +561,25 @@
                     total = total + far[a, k - 1, :, 0:n].astype(F32)
                 src[here, :] = total.astype(BF)
             for k in peers(last):
-                up(last, k, levels[last][1]).start()
+                up(last, k).start()
             local().start()
 
         def step_up(j):
             if j == last:
                 local().wait()
-            for k in peers(j):
-                up(j, k, from_pos(j, k)).wait_recv()
+            all_up(j).wait_recv()
             if j == 0:
                 core_up(core).start()
             else:
                 for k in peers(j - 1):
-                    up(j - 1, k, levels[j - 1][1]).start()
+                    up(j - 1, k).start()
 
         def step_last():
             core_up(1 - core).wait_recv()
 
         def step_sent():
-            core_send().wait_send()
-            core_up(core).wait_send()
-            for j in range(last + 1):
-                for k in peers(j):
-                    down(j, k).wait_send()
-                    up(j, k, levels[j][1]).wait_send()
+            all_sent(0).wait_send()
+            all_sent(1).wait_send()
 
         steps = [step_core] + [functools.partial(step_down, j) for j in range(last + 1)] + [step_turn]
         return steps + [functools.partial(step_up, j) for j in range(last, -1, -1)] + [step_last, step_sent]
@@ -588,16 +611,16 @@
             return copy(small_s.at[0, other], small_c, 0, core_peer)
 
         def plane_send(k):
-            return copy(small_s.at[1, mine], small_p.at[k - 1], k, plane_peer(k))
+            return copy(small_s.at[1, mine], small_p.at[k - 1], 1, plane_peer(k))
 
         def z_send(k):
-            return copy(small_s.at[2, mine], small_z.at[k - 1], 3 + k, z_peer(k))
+            return copy(small_s.at[2, mine], small_z.at[k - 1], 2, z_peer(k))
 
         def far_copy(k):
-            return copy(small_s.at[3, mine], small_far.at[k - 1], 7 + k, far_peer(k))
+            return copy(small_s.at[3, mine], small_far.at[k - 1], 3 + k, far_peer(k))
 
         def core_up(rows):
-            return copy(small_o.at[rows], small_o.at[rows], 7, core_peer)
+            return copy(small_o.at[rows], small_o.at[rows], 3, core_peer)
 
         def step0():
             core_send().start()
@@ -610,18 +633,18 @@
 
         def step2():
             total = small_s[1, mine, :]
-            for k in range(1, 4):
-                plane_send(k).wait_recv()
-                total = total + small_p[k - 1]
+            copy(small_p, small_p, 1, core_peer).wait_recv()
+            for k in range(3):
+                total = total + small_p[k]
             small_s[2, mine, :] = total
             for k in range(1, 4):
                 z_send(k).start()
 
         def step3():
             total = small_s[2, mine, :]
-            for k in range(1, 4):
-                z_send(k).wait_recv()
-                total = total + small_z[k - 1]
+            copy(small_z, small_z, 2, core_peer).wait_recv()
+            for k in range(3):
+                total = total + small_z[k]
             if extra > 1:
                 small_s[3, mine, :] = total
                 for k in range(1, extra):
@@ -639,9 +662,8 @@
         def step5():
             core_send().wait_send()
             core_up(mine).wait_send()
-            for k in range(1, 4):
-                plane_send(k).wait_send()
-                z_send(k).wait_send()
+            copy(small_p, small_p, 1, core_peer).wait_send()
+            copy(small_z, small_z, 2, core_peer).wait_send()
 
         return [step0, step1, step2, step3, step4, step5]
 
@@ -841,20 +863,28 @@
 
     lax.fori_loop(0, 4, net_back, 0)
     run("net")
-    run("end")
-
-    for group in groups:
-        group[-1]()
-    own_res.wait()
-    own_gin.wait()
     for k in (1, 2, 3):
-        frm, to = ring_from(k), lax.rem(me + k, n_win)
+        frm = ring_from(k)
         x_send(k, 0).wait_send()
         x_send(k, 1).wait_send()
         spread(cot_hbm, cr, s_c, r_c, k).wait_send()
-        res_copy(to).wait_send()
+        res_copy(lax.rem(me + k, n_win)).wait_send()
+        remote(xr.at[frm], res_hbm.at[frm, 0], s_res.at[frm], r_res.at[frm], (img, frm)).wait_recv()
+    own_res.wait()
+    own_gin.wait()
+    last = {at: j for at, j in SCHEDULE["end"]}
+    late = [at for at, group in enumerate(groups) if last.get(at) == len(group) - 2]
+    for at, group in enumerate(groups):
+        if at not in late:
+            group[-1]()
+    for at, j in SCHEDULE["end"]:
+        groups[at][j]()
+        if at in late and j == len(groups[at]) - 2:
+            groups[at][-1]()
+
+    for k in (1, 2, 3):
+        frm, to = ring_from(k), lax.rem(me + k, n_win)
         gin_copy(to).wait_send()
-        remote(xr.at[frm], res_hbm.at[frm, 0], s_res.at[frm], r_res.at[frm], (img, frm)).wait_recv()
         remote(slope.at[frm], gin_hbm.at[frm, 0], s_gin.at[frm], r_gin.at[frm], (img, frm)).wait_recv()
 
 
@@ -899,7 +929,7 @@
     for c in range(4):
         g_be[512 * c : 512 * c + 512] = small[ROW_BE + c, :]
     g_w1[...] = small[ROW_W1 : ROW_W1 + 2, :]
-    g_w2[...] = small[ROW_W2 : ROW_W2 + 16, :].T
+    g_w2[...] = small[ROW_W2 : ROW_W2 + 16, :]
     h0 = lax.broadcasted_iota(jnp.int32, (512, 16), 0) // 32
     h1 = lax.broadcasted_iota(jnp.int32, (512, 16), 1)
     heads = jnp.where(h0 == h1, 1.0, 0.0).astype(BF)
@@ -911,10 +941,9 @@
 
 def body(n_img, n_win, inputs, wqkv, qb, vb, hls, w1, b1, w2, wproj, bproj, g1, s1, we, be, wc, bc, g2, s2, cot):
     extra = n_img // 8
-    crow, ccol = table_coords()
+    crow = table_coords()
     dma = pltpu.SemaphoreType.DMA
-    n_ar = 15 + (extra - 1)
-    n_sm = 8 + (extra - 1)
+    n_sm = 4 + (extra - 1)
     vmem = pl.BlockSpec(memory_space=pltpu.VMEM)
     hbm = pl.BlockSpec(memory_space=pl.ANY)
     smem = pl.BlockSpec(memory_space=pltpu.SMEM)
@@ -949,6 +978,11 @@
         pltpu.VMEM((512, 512), BF),
         pltpu.VMEM((512, 2048), BF),
         pltpu.VMEM((2048, 512), BF),
+        pltpu.VMEM((512,), F32), pltpu.VMEM((512,), F32),
+        pltpu.VMEM((2, 512), F32), pltpu.VMEM((512,), F32), pltpu.VMEM((16, 512), F32),
+        pltpu.VMEM((512,), F32), pltpu.VMEM((512,), F32), pltpu.VMEM((512,), F32),
+        pltpu.VMEM((2048,), F32), pltpu.VMEM((512,), F32),
+        pltpu.VMEM((512,), F32), pltpu.VMEM((512,), F32), pltpu.VMEM((8, 1024), F32),
         pltpu.VMEM((4, SMALL_ROWS, 512), F32),
         pltpu.VMEM((16, 512), F32),
         pltpu.VMEM((3, 16, 512), F32),
@@ -957,9 +991,9 @@
         pltpu.VMEM((SMALL_ROWS, 512), F32),
         dma((2, 4)), dma((2, 4)), dma((4,)), dma((4,)),
         dma((4,)), dma((4,)), dma((4,)), dma((4,)),
-        dma((15, n_ar)), dma((15, n_ar)), dma((15,)),
+        dma((15, 1 + extra)), dma((15, 9 + extra)), dma((15,)),
         dma((n_sm,)), dma((n_sm,)),
-        dma((4,)),
+        dma((4,)), dma((13,)),
     ]
     block = jax.ShapeDtypeStruct(inputs.shape, BF)
     result, grad_inputs, wide, qkv, small = pl.pallas_call(
@@ -971,22 +1005,22 @@
             jax.ShapeDtypeStruct((2, 3, 512, 256), BF),
             jax.ShapeDtypeStruct((SMALL_ROWS, 512), F32),
         ),
-        in_specs=[hbm] * 6 + [vmem] * 2 + [smem] + [vmem] * 12,
+        in_specs=[hbm] * 6 + [smem] + [hbm] * 13,
         out_specs=(hbm, hbm, hbm, hbm, vmem),
         scratch_shapes=scratch,
         compiler_params=pltpu.CompilerParams(
             collective_id=0, has_side_effects=True, vmem_limit_bytes=64 * 1024 * 1024
         ),
     )(
-        inputs, cot, wqkv, wproj, we, wc, qb, vb, hls, w1, b1, w2.T, bproj, g1, s1, be, bc, g2, s2,
-        jnp.asarray(crow), jnp.asarray(ccol),
+        inputs, cot, wqkv, wproj, we, wc, hls, qb, vb, w1, b1, w2.T, bproj, g1, s1, be, bc, g2, s2,
+        jnp.asarray(crow),
     )
     any_ = lambda shape: jax.ShapeDtypeStruct(shape, F32)
     outs = pl.pallas_call(
         widen_kernel,
         out_shape=(
             block, block, any_((512, 1536)), any_((512,)), any_((512,)), any_((16,)), any_((2, 512)),
-            any_((512,)), any_((512, 16)), any_((512, 512)), any_((512,)), any_((512,)), any_((512,)),
+            any_((512,)), any_((16, 512)), any_((512, 512)), any_((512,)), any_((512,)), any_((512,)),
             any_((512, 2048)), any_((2048,)), any_((2048, 512)), any_((512,)), any_((512,)), any_((512,)),
         ),
         in_specs=[hbm] * 4 + [vmem],
@@ -1001,7 +1035,7 @@
         ],
         compiler_params=pltpu.CompilerParams(vmem_limit_bytes=63 * 1024 * 1024),
     )(result, grad_inputs, wide, qkv, small)
-    return outs
+    return outs[:8] + (outs[8].T,) + outs[9:]
 
 
 def solution(mesh):

time: 133 us -> 127 us (0.955)
  Pallas kernels: 131 us -> 126 us
  local copies, waits for them, and re-layouts: 1.67 us -> 0 us
    pallas_call x1, Pallas kernels: 121 us -> 117 us  [body(): pl.pallas_call(functools.partial(block_kernel, n_img, n_win), out_shape=(...]
    pallas_call x1 -> x0, local copies, waits for them, and re-layouts: 1.67 us -> none  [body(): pl.pallas_call(widen_kernel, out_shape=(block, block, any_((512, 1536)),...]
where the time goes in v3:
time: 127 us
  Pallas kernels  126 us (99%)
    pallas_call x1, Pallas kernels, body(): pl.pallas_call(functools.partial(block_kernel, n_img, n_win), out_shape=(...  117 us
    pallas_call x1, Pallas kernels, body(): pl.pallas_call(widen_kernel, out_shape=(block, block, any_((512, 1536)),...  9.44 us

profile of v3, /device:TPU:0, one launch (start us, length us, event | category | flops | bytes accessed | tf_op | source)
XLA Modules:
  0.0 127.2 jit_solution(11509351812206344166)
XLA Ops:
  0.7 117.0 %shard_map.339 = (bf16[4,1,256,512]{3,2,1,0:T(8,128)(2,1)}, bf16[4,1,256,512]{3,2,1,0:T(8,128)(2,1)}, bf16[9,512,512]{2,1,0:T(8,128)(2,1)}, bf16[2,3,512,256]{3,2,1,0:T(8,128)(2,1)}, f32[32,512]{1,0:T(8,128)}) custom-call(bf16[4,1,256,512]{3,2,1,0:T(8,128)(2,1)} %x_hbm.1, bf16[4,1,256,512]{3,2,1,0:T(8,128)(2,1)} %cot_hbm.1, bf16[512,1536]{1,0:T(8,128)(2,1)} %wqkv_hbm.1, ...), custom_call_target="tpu_custom_call" | custom-call | tf_op jit(solution)/shard_map/pallas_call | solution.py:999
  117.6 9.4 %shard_map.340 = (bf16[4,1,256,512]{3,2,1,0:T(8,128)(2,1)}, bf16[4,1,256,512]{3,2,1,0:T(8,128)(2,1)}, f32[512,1536]{1,0:T(8,128)}, f32[512]{0:T(512)}, f32[512]{...) custom-call(bf16[4,1,256,512]{3,2,1,0:T(8,128)(2,1)} %get-tuple-elem, ...), custom_call_target="tpu_custom_call" | custom-call | tf_op jit(solution)/shard_map/pallas_call | solution.py:1019

commit v4 on v3

--- a/solution.py
+++ b/solution.py
@@ -30,27 +30,31 @@
     "d0": ((1, 1),),
     "d1": ((2, 0), (0, 2)),
     "d2": ((2, 1), (1, 2)),
-    "d3": ((3, 0), (0, 3)),
-    "nb": ((3, 1), (2, 2)),
-    "gproj": ((4, 0), (1, 3), (0, 4)),
-    "r0": ((4, 1), (0, 5), (2, 3), (1, 4)),
-    "r1": ((3, 2),),
-    "r2": ((1, 5), (4, 2), (2, 4), (0, 6)),
-    "r3": ((3, 3),),
-    "gq0": ((5, 0), (1, 6), (4, 3), (2, 5), (5, 1), (3, 4)),
-    "r4": ((0, 7), (1, 7)),
-    "r5": ((4, 4), (5, 2), (2, 6), (3, 5), (1, 8)),
-    "r6": ((0, 8),),
-    "r7": ((4, 5), (5, 3), (2, 7)),
-    "gq1": ((6, 0), (3, 6), (4, 6), (1, 9), (6, 1), (5, 4), (1, 10), (0, 9), (3, 7)),
-    "finish": ((2, 8), (0, 10)),
-    "bb": ((6, 2), (5, 5), (3, 8)),
-    "net": ((7, 0), (2, 9), (7, 1)),
-    "end": ((6, 3), (2, 10), (3, 9), (5, 6), (3, 10), (6, 4), (7, 2), (5, 7), (5, 8), (7, 3), (6, 5), (7, 4), (6, 6)),
+    "d3": ((3, 0),),
+    "nb": ((0, 3), (3, 1)),
+    "gproj": ((4, 0), (2, 2)),
+    "r0": ((4, 1), (1, 3), (3, 2)),
+    "r1": ((0, 4),),
+    "r2": ((2, 3), (4, 2), (1, 4)),
+    "r3": ((3, 3), (0, 5), (2, 4)),
+    "gq0": ((5, 0), (4, 3)),
+    "r4": ((5, 1), (3, 4), (2, 5), (0, 6)),
+    "r5": ((4, 4),),
+    "r6": ((1, 5), (5, 2), (3, 5)),
+    "r7": ((2, 6), (0, 7)),
+    "gq1": ((6, 0), (4, 5), (1, 6), (5, 3), (0, 8), (3, 6), (6, 1), (2, 7)),
+    "finish": ((4, 6),),
+    "puts": ((1, 7), (5, 4)),
+    "bb": ((3, 7), (6, 2), (2, 8)),
+    "net": ((7, 0), (1, 8), (5, 5), (7, 1), (3, 8)),
+    "end": (
+        (6, 3), (2, 9), (2, 10), (1, 9), (5, 6), (7, 2), (1, 10), (6, 4), (3, 9), (5, 7), (3, 10), (5, 8), (7, 3),
+        (6, 5), (7, 4), (6, 6),
+    ),
 }
 ORDERS = (
-    "wvxy", "xwvy", "xywv", "yxwv", "xywv", "wvxy", "xwyv", "xwyv", "pz",
-    "xzy", "yxz", "xzy", "pz", "pz", "pz",
+    "wpv", "xyz", "wvxy", "xwyv", "wvxy", "xwyv", "xwvy", "yxwv", "pz",
+    "pwv", "wpv", "wpv", "pz", "pz", "pz",
 )
 
 

time: 127 us -> 123 us (0.969)
  Pallas kernels: 126 us -> 122 us
    pallas_call x1, Pallas kernels: 117 us -> 113 us  [body(): pl.pallas_call(functools.partial(block_kernel, n_img, n_win), out_shape=(...]
where the time goes in v4:
time: 123 us
  Pallas kernels  122 us (99%)
    pallas_call x1, Pallas kernels, body(): pl.pallas_call(functools.partial(block_kernel, n_img, n_win), out_shape=(...  113 us
    pallas_call x1, Pallas kernels, body(): pl.pallas_call(widen_kernel, out_shape=(block, block, any_((512, 1536)),...  9.44 us

profile of v4, /device:TPU:0, one launch (start us, length us, event | category | flops | bytes accessed | tf_op | source)
XLA Modules:
  0.0 123.3 jit_solution(3954738345353926227)
XLA Ops:
  0.7 113.0 %shard_map.339 = (bf16[4,1,256,512]{3,2,1,0:T(8,128)(2,1)}, bf16[4,1,256,512]{3,2,1,0:T(8,128)(2,1)}, bf16[9,512,512]{2,1,0:T(8,128)(2,1)}, bf16[2,3,512,256]{3,2,1,0:T(8,128)(2,1)}, f32[32,512]{1,0:T(8,128)}) custom-call(bf16[4,1,256,512]{3,2,1,0:T(8,128)(2,1)} %x_hbm.1, bf16[4,1,256,512]{3,2,1,0:T(8,128)(2,1)} %cot_hbm.1, bf16[512,1536]{1,0:T(8,128)(2,1)} %wqkv_hbm.1, ...), custom_call_target="tpu_custom_call" | custom-call | tf_op jit(solution)/shard_map/pallas_call | solution.py:1003
  113.7 9.4 %shard_map.340 = (bf16[4,1,256,512]{3,2,1,0:T(8,128)(2,1)}, bf16[4,1,256,512]{3,2,1,0:T(8,128)(2,1)}, f32[512,1536]{1,0:T(8,128)}, f32[512]{0:T(512)}, f32[512]{...) custom-call(bf16[4,1,256,512]{3,2,1,0:T(8,128)(2,1)} %get-tuple-elem, ...), custom_call_target="tpu_custom_call" | custom-call | tf_op jit(solution)/shard_map/pallas_call | solution.py:1023

commit v5 on v4

--- a/solution.py
+++ b/solution.py
@@ -251,9 +251,9 @@
         part[:, u, :] = pltpu.roll(tab[...], 1001 + u, 1)
     pick = one_hot_pick()
     short = jnp.concatenate(
-        [sum(nn(p, pick) for p in split3(part[4 * i : 4 * i + 4].reshape(96, 1024))) for i in range(4)], axis=0
+        [sum(nn(p, pick) for p in split3(part[4 * i : 4 * i + 4].reshape(96, 1024))[:2]) for i in range(4)], axis=0
     )
-    short_parts = split3(short)
+    short_parts = split3(short)[:2]
     for c in range(4):
         places = one_hot_places(c)
         wide = sum(nn(p, places) for p in short_parts)

time: 123 us -> 123 us (level)
  no operation moved by 1% of the time
where the time goes in v5:
time: 123 us
  Pallas kernels  122 us (99%)
    pallas_call x1, Pallas kernels, body(): pl.pallas_call(functools.partial(block_kernel, n_img, n_win), out_shape=(...  113 us
    pallas_call x1, Pallas kernels, body(): pl.pallas_call(widen_kernel, out_shape=(block, block, any_((512, 1536)),...  9.44 us

profile of v5, /device:TPU:0, one launch (start us, length us, event | category | flops | bytes accessed | tf_op | source)
XLA Modules:
  0.0 123.0 jit_solution(6604225061012262726)
XLA Ops:
  0.7 112.8 %shard_map.339 = (bf16[4,1,256,512]{3,2,1,0:T(8,128)(2,1)}, bf16[4,1,256,512]{3,2,1,0:T(8,128)(2,1)}, bf16[9,512,512]{2,1,0:T(8,128)(2,1)}, bf16[2,3,512,256]{3,2,1,0:T(8,128)(2,1)}, f32[32,512]{1,0:T(8,128)}) custom-call(bf16[4,1,256,512]{3,2,1,0:T(8,128)(2,1)} %x_hbm.1, bf16[4,1,256,512]{3,2,1,0:T(8,128)(2,1)} %cot_hbm.1, bf16[512,1536]{1,0:T(8,128)(2,1)} %wqkv_hbm.1, ...), custom_call_target="tpu_custom_call" | custom-call | tf_op jit(solution)/shard_map/pallas_call | solution.py:1003
  113.4 9.4 %shard_map.340 = (bf16[4,1,256,512]{3,2,1,0:T(8,128)(2,1)}, bf16[4,1,256,512]{3,2,1,0:T(8,128)(2,1)}, f32[512,1536]{1,0:T(8,128)}, f32[512]{0:T(512)}, f32[512]{...) custom-call(bf16[4,1,256,512]{3,2,1,0:T(8,128)(2,1)} %get-tuple-elem, ...), custom_call_target="tpu_custom_call" | custom-call | tf_op jit(solution)/shard_map/pallas_call | solution.py:1023
